TPU v7x, 256 devices: a whole 4x4x8 slice. The times are simulated.
256 devices in a mesh: segment: 4 (over y_lo, core), tp: 64 (over x, y_hi, z).
Axes of the slice: x: 4, y: 4 (y_hi: 2, y_lo: 2; y = y_hi * 2 + y_lo), z: 8, core: 2. Of those that a mesh axis runs over, the one named last changes fastest.
Arguments:
- top_grad: bfloat16 [2, 128, 4096], P(None, None, 'tp'), may hold values from -6 to 6
- saved_in: bfloat16 [2, 4, 128, 4096], P(None, 'segment', None, 'tp'), may hold values from -6 to 6
- saved_pre: bfloat16 [2, 4, 128, 16384], P(None, 'segment', None, 'tp'), may hold values from -6 to 6
- w_up: bfloat16 [2, 4, 4096, 16384], P(None, 'segment', None, 'tp'), as said below
- w_down: bfloat16 [2, 4, 16384, 4096], P(None, 'segment', 'tp'), as said below
- mask_up: int32 [2, 4, 32, 128], P(None, 'segment', None, 'tp'), may hold values from 0 to 1, as said below
- mask_down: int32 [2, 4, 128, 32], P(None, 'segment', 'tp'), may hold values from 0 to 1, as said below
Outputs:
- all_grads: bfloat16 [2, 4, 128, 4096], P(None, 'segment', None, 'tp')
- grad_up: bfloat16 [2, 4, 2048, 16384], P(None, 'segment', None, 'tp')
- grad_down: bfloat16 [2, 4, 16384, 2048], P(None, 'segment', 'tp')
Inputs may be any that keep to these rules, and one draw needn't show every extreme that they name: `mask_up`: 0 or 1; in every row, of each aligned pair of blocks along the hidden units (blocks 2j and 2j + 1) exactly one is 1; entry [1, s] equals entry [0, 3 - s]. `mask_down`: 0 or 1; in every column, of each aligned pair of blocks along the hidden units (blocks 2j and 2j + 1) exactly one is 1; entry [1, s] equals entry [0, 3 - s]. `w_up`: entry [1, s] equals entry [0, 3 - s]. `w_down`: entry [1, s] equals entry [0, 3 - s].
All inputs are finite; a program needn't handle non-finite values.
Results may differ from a plain program's by a relative error of at most 0.017.
Values may be sent and summed in bfloat16 or wider, within the bound.
No kernel may reach another device: no remote copies, remote signals or barrier semaphores. Data moves between devices by JAX's collectives and lax.ppermute only.
A program may use at most 128 MiB of HBM per device.

v0:
```python
import functools

import jax
import jax.numpy as jnp
from jax import lax
from jax.experimental import pallas as pl
from jax.experimental.pallas import tpu as pltpu
from jax.sharding import PartitionSpec as P

BLOCK = 128
F32 = jnp.float32
BF16 = jnp.bfloat16
VMEM_BYTES = 40 << 20
NT = (((1,), (1,)), ((), ()))


def swap(value, bits):
    return lax.ppermute(value, "segment", [(s, s ^ bits) for s in range(4)])


def exchange(parts):
    return lax.all_to_all(parts, "tp", 0, 0, tiled=True)


def pick(condition, a, b):
    return jnp.where(condition, a, b)


def at(stack, i):
    return lax.dynamic_index_in_dim(stack, i, 0, keepdims=False)


def kept_blocks(value, mask):
    return jnp.where(mask > 0, value, jnp.zeros_like(value))


def params():
    return pltpu.CompilerParams(vmem_limit_bytes=VMEM_BYTES)


def prepare_kernel(share, info, mask_u, mask_d, up, down, keep_d, send_d, keep_u, send_u):
    which, core, woven = info[0], info[1], info[2]
    half = keep_u.shape[0]
    blocks = half // BLOCK
    pairs = up.shape[3] // BLOCK

    def columns(b, carry):
        for out, c in ((keep_d, core), (send_d, 1 - core)):
            block = c * blocks + b
            source = pl.ds(pl.multiple_of(block * BLOCK, BLOCK), BLOCK)
            target = pl.ds(pl.multiple_of(b * BLOCK, BLOCK), BLOCK)
            for h in range(pairs):
                rows = slice(h * BLOCK, (h + 1) * BLOCK)
                out[rows, target] = kept_blocks(down[0, 0, rows, source], mask_d[(which * pairs + h) * 2 * blocks + block])
        return carry

    def rows(j, carry):
        for out, c in ((keep_u, core), (send_u, 1 - core)):
            first = jnp.where(woven > 0, (2 * j + c) * share, c * half + j * share)
            source = pl.ds(pl.multiple_of(first, share), share)
            target = pl.ds(pl.multiple_of(j * share, share), share)
            block = first // BLOCK
            for h in range(pairs):
                lanes = slice(h * BLOCK, (h + 1) * BLOCK)
                out[target, lanes] = kept_blocks(up[0, 0, source, lanes], mask_u[(which * 2 * blocks + block) * pairs + h])
        return carry

    lax.fori_loop(0, blocks, columns, 0, unroll=2)
    lax.fori_loop(0, half // share, rows, 0, unroll=4)


def prepare(info, mask_u, mask_d, w_up, w_down, share):
    _, _, features, hidden = w_up.shape
    half = features // 2
    whole = lambda shape: pl.BlockSpec(shape, lambda i, *_: (0, 0))
    return pl.pallas_call(
        functools.partial(prepare_kernel, share),
        grid_spec=pltpu.PrefetchScalarGridSpec(
            num_scalar_prefetch=3,
            grid=(1,),
            in_specs=[
                pl.BlockSpec((1, 1, features, hidden), lambda i, info, *_: (info[0], 0, 0, 0)),
                pl.BlockSpec((1, 1, hidden, features), lambda i, info, *_: (info[0], 0, 0, 0)),
            ],
            out_specs=[whole((hidden, half))] * 2 + [whole((half, hidden))] * 2,
        ),
        out_shape=[jax.ShapeDtypeStruct((hidden, half), BF16)] * 2 + [jax.ShapeDtypeStruct((half, hidden), BF16)] * 2,
        compiler_params=params(),
        cost_estimate=pl.CostEstimate(flops=0, bytes_accessed=8 * features * hidden, transcendentals=0),
        name="prepare",
    )(info, mask_u, mask_d, w_up, w_down)


def fetch(flag, keep, came, held, sem, act):
    for wanted, source in ((1, keep), (0, came)):

        @pl.when(flag[0] == wanted)
        def _(source=source):
            copy = pltpu.make_async_copy(source, held, sem)
            copy.start() if act == "start" else copy.wait()


def down_kernel(flag, keep, came, grad, out, held, sem):
    fetch(flag, keep, came, held, sem, "start")
    fetch(flag, keep, came, held, sem, "wait")
    out[...] = jnp.dot(held[...], grad[...], preferred_element_type=F32)


def down_step(flag, keep, came, grad):
    hidden, half = keep.shape
    tokens = grad.shape[1]
    return pl.pallas_call(
        down_kernel,
        in_specs=[pl.BlockSpec(memory_space=pltpu.SMEM)] + [pl.BlockSpec(memory_space=pl.ANY)] * 2 + [pl.BlockSpec(memory_space=pltpu.VMEM)],
        out_specs=pl.BlockSpec(memory_space=pltpu.VMEM),
        out_shape=jax.ShapeDtypeStruct((hidden, tokens), F32),
        scratch_shapes=[pltpu.VMEM((hidden, half), BF16), pltpu.SemaphoreType.DMA],
        compiler_params=params(),
        cost_estimate=pl.CostEstimate(flops=2 * hidden * half * tokens, bytes_accessed=2 * hidden * half, transcendentals=0),
        name="down",
    )(flag, keep, came, grad)


def up_kernel(flag, keep, came, part, peer, pre, du_out, out, held, sem):
    fetch(flag, keep, came, held, sem, "start")
    u = pre[...].astype(F32)
    sig = jax.nn.sigmoid(u)
    du = ((part[...] + peer[...]) * sig * (1.0 + u * (1.0 - sig))).astype(BF16)
    du_out[...] = du
    fetch(flag, keep, came, held, sem, "wait")
    rows = min(512, out.shape[0])
    for i in range(out.shape[0] // rows):
        at_rows = slice(i * rows, (i + 1) * rows)
        out[at_rows] = jnp.dot(held[at_rows], du, preferred_element_type=F32).astype(BF16)


def up_step(flag, keep, came, part, peer, pre):
    half, hidden = keep.shape
    tokens = part.shape[1]
    vmem = pl.BlockSpec(memory_space=pltpu.VMEM)
    return pl.pallas_call(
        up_kernel,
        in_specs=[pl.BlockSpec(memory_space=pltpu.SMEM)] + [pl.BlockSpec(memory_space=pl.ANY)] * 2 + [vmem] * 3,
        out_specs=[vmem] * 2,
        out_shape=[jax.ShapeDtypeStruct((hidden, tokens), BF16), jax.ShapeDtypeStruct((half, tokens), BF16)],
        scratch_shapes=[pltpu.VMEM((half, hidden), BF16), pltpu.SemaphoreType.DMA],
        compiler_params=params(),
        cost_estimate=pl.CostEstimate(flops=2 * hidden * half * tokens, bytes_accessed=2 * hidden * half, transcendentals=hidden * tokens),
        name="up",
    )(flag, keep, came, part, peer, pre)


def up_grad_kernel(mask_u, x, du, out):
    i = pl.program_id(0)
    rows, hidden = out.shape[2], out.shape[3]
    pairs = hidden // BLOCK
    steps = pl.num_programs(0)
    both = jnp.concatenate([x[0], x[1]], axis=1)
    total = lax.dot_general(both, du[0], NT, preferred_element_type=F32)
    layer = i // (steps // 2)
    blocks = steps * rows // BLOCK
    for b in range(rows // BLOCK):
        at_rows = slice(b * BLOCK, (b + 1) * BLOCK)
        block = i * (rows // BLOCK) + b
        for h in range(pairs):
            lanes = slice(h * BLOCK, (h + 1) * BLOCK)
            out[0, 0, at_rows, lanes] = kept_blocks(total[at_rows, lanes], mask_u[(layer * blocks + block) * pairs + h]).astype(BF16)


def up_grads(mask_u, x, du):
    _, features, tokens = x.shape
    hidden = du.shape[1]
    half = features // 2
    rows = min(512, half)
    per = half // rows
    return pl.pallas_call(
        up_grad_kernel,
        grid_spec=pltpu.PrefetchScalarGridSpec(
            num_scalar_prefetch=1,
            grid=(2 * per,),
            in_specs=[
                pl.BlockSpec((2, rows, tokens), lambda i, _: (0, i, 0)),
                pl.BlockSpec((1, hidden, 2 * tokens), lambda i, _: (i // per, 0, 0)),
            ],
            out_specs=pl.BlockSpec((1, 1, rows, hidden), lambda i, _: (i // per, 0, i % per, 0)),
        ),
        out_shape=jax.ShapeDtypeStruct((2, 1, half, hidden), BF16),
        compiler_params=params(),
        cost_estimate=pl.CostEstimate(flops=4 * features * hidden * tokens, bytes_accessed=4 * features * hidden, transcendentals=0),
        name="up_grads",
    )(mask_u, x, du)


def down_grad_kernel(mask_d, core, h, here, across, sibling, partner, out):
    pair, i = pl.program_id(0), pl.program_id(1)
    hidden, columns = out.shape[2], out.shape[3]
    pairs = hidden // BLOCK
    half_blocks = pl.num_programs(1) * columns // BLOCK
    layer = jnp.where(pair == 0, core[0], 1 - core[0])

    def write(a, b):
        both = jnp.concatenate([a[...], b[...]], axis=1)
        total = lax.dot_general(h[0], both, NT, preferred_element_type=F32)
        for k in range(columns // BLOCK):
            lanes = slice(k * BLOCK, (k + 1) * BLOCK)
            block = layer * half_blocks + i * (columns // BLOCK) + k
            for p in range(pairs):
                rows = slice(p * BLOCK, (p + 1) * BLOCK)
                mask = mask_d[(layer * pairs + p) * 2 * half_blocks + block]
                out[0, 0, rows, lanes] = kept_blocks(total[rows, lanes], mask).astype(BF16)

    @pl.when(pair == 0)
    def _():
        write(here, across)

    @pl.when(pair == 1)
    def _():
        write(sibling, partner)


def down_grads(mask_d, core, h, here, across, sibling, partner):
    half, tokens = here.shape
    hidden = h.shape[1]
    columns = min(512, half)
    per = half // columns
    first = pl.BlockSpec((columns, tokens), lambda p, i, *_: (jnp.where(p == 0, i, per - 1), 0))
    second = pl.BlockSpec((columns, tokens), lambda p, i, *_: (jnp.where(p == 0, 0, i), 0))
    return pl.pallas_call(
        down_grad_kernel,
        grid_spec=pltpu.PrefetchScalarGridSpec(
            num_scalar_prefetch=2,
            grid=(2, per),
            in_specs=[pl.BlockSpec((1, hidden, 2 * tokens), lambda p, i, *_: (p, 0, 0)), first, first, second, second],
            out_specs=pl.BlockSpec(
                (1, 1, hidden, columns), lambda p, i, _, core: (jnp.where(p == 0, core[0], 1 - core[0]), 0, 0, i)
            ),
        ),
        out_shape=jax.ShapeDtypeStruct((2, 1, hidden, half), BF16),
        compiler_params=params(),
        cost_estimate=pl.CostEstimate(flops=8 * half * hidden * tokens, bytes_accessed=8 * half * hidden, transcendentals=0),
        name="down_grads",
    )(mask_d, core, h, here, across, sibling, partner)


def per_device(top_grad, saved_in, saved_pre, w_up, w_down, mask_up, mask_down):
    members = lax.axis_size("tp")
    section = lax.axis_index("segment")
    place = lax.axis_index("tp")
    core = section & 1
    rep = section >> 1
    outer = (core ^ rep) == 0
    even = core == 0
    near = rep == 0
    features = w_up.shape[2]
    half = features // 2
    share = half // members
    tokens = top_grad.shape[1]

    mine = at(at(top_grad, rep).T.reshape(2, share, tokens), core)
    got = exchange(jnp.broadcast_to(mine[None], (members, share, tokens))).reshape(2, members // 2, share, tokens)

    xs = saved_in[:, 0].transpose(0, 2, 1)
    x_far0, x_far1 = swap(xs[0], 3), swap(xs[1], 3)
    low_member = place < members // 2
    x_sent = jnp.stack([pick(low_member, xs[0], x_far0), pick(low_member, x_far1, xs[1])])
    x_full = lax.all_gather(x_sent, "tp", axis=1, tiled=True)

    pre = saved_pre[:, 0].transpose(0, 2, 1)
    pre_partner = swap(pre, 3)
    pre_across = swap(at(pre, 1 - rep), 2)
    pre_sibling = swap(at(pre, rep), 1)

    mask_u, mask_d = mask_up.reshape(-1), mask_down.reshape(-1)
    zero = jnp.zeros((), jnp.int32)
    first_info = jnp.stack([1 - rep, core, zero])
    second_info = jnp.stack([rep, core, outer.astype(jnp.int32)])
    keep_d1, send_d1, keep_u1, send_u1 = prepare(first_info, mask_u, mask_d, w_up, w_down, share)
    came_d1, came_u1 = swap(send_d1, 1), swap(send_u1, 1)
    keep_d2, send_d2, keep_u2, send_u2 = prepare(second_info, mask_u, mask_d, w_up, w_down, share)
    came_d2, came_u2 = swap(send_d2, 1), swap(send_u2, 1)
    at_outer = outer.astype(jnp.int32)[None]
    weights = {
        3: (at_outer, keep_d1, came_d1, keep_u1, came_u1),
        2: (1 - at_outer, keep_d1, came_d1, keep_u1, came_u1),
        1: (1 - at_outer, keep_d2, came_d2, keep_u2, came_u2),
        0: (at_outer, keep_d2, came_d2, keep_u2, came_u2),
    }
    pre_first, pre_second = at(pre_partner, rep), at(pre, rep)
    pre_of = {
        3: pick(outer, pre_first, pre_across),
        2: pick(outer, pre_across, pre_first),
        1: pick(outer, pre_sibling, pre_second),
        0: pick(outer, pre_second, pre_sibling),
    }

    kept = at(got, core)
    traded = swap(at(got, 1 - core), 1)
    grad = pick(even, jnp.stack([kept, traded], 1), jnp.stack([traded, kept], 1)).reshape(half, tokens)

    grads, dus, shards = {}, {}, {}
    for layer in (3, 2, 1, 0):
        grads[layer] = grad
        flag, keep_d, came_d, keep_u, came_u = weights[layer]
        partial = down_step(flag, keep_d, came_d, grad)
        dus[layer], out = up_step(flag, keep_u, came_u, partial, swap(partial, 1), pre_of[layer])
        landed = exchange(out.reshape(members, share, tokens))
        total = jnp.sum(landed.astype(F32), axis=0)
        if layer:
            own = lax.dynamic_slice_in_dim(grad, place * share, share, 0)
            out = (own.astype(F32) + total).astype(BF16)
            grad = exchange(jnp.broadcast_to(out[None], (members, share, tokens))).reshape(half, tokens)
            mine = lax.dynamic_slice_in_dim(grad, (place % (members // 2)) * 2 * share, 2 * share, 0)
            shards[layer] = pick(place // (members // 2) == core, mine, swap(mine, 1))
        else:
            own = lax.dynamic_slice_in_dim(shards[1], core * share, share, 0)
            out = (own.astype(F32) + total).astype(BF16)
            peer = swap(out, 1)
            shards[0] = pick(even, jnp.concatenate([out, peer]), jnp.concatenate([peer, out]))

    own_out = pick(outer, shards[0], shards[1])
    far_out = swap(pick(outer, shards[2], shards[3]), 2)
    all_grads = pick(near, jnp.stack([own_out, far_out]), jnp.stack([far_out, own_out]))
    all_grads = all_grads.transpose(0, 2, 1)[:, None]

    first_du, second_du = pick(outer, dus[3], dus[2]), pick(outer, dus[0], dus[1])
    far_first, far_second = swap(first_du, 3), swap(second_du, 3)
    low_own, low_far = pick(near, second_du, first_du), pick(near, far_second, far_first)
    high_own, high_far = pick(near, first_du, second_du), pick(near, far_first, far_second)
    du_low = jnp.concatenate([pick(near, low_own, low_far), pick(near, low_far, low_own)], 1)
    du_high = jnp.concatenate([pick(near, high_own, high_far), pick(near, high_far, high_own)], 1)
    grad_up = up_grads(mask_u, x_full, jnp.stack([du_low, du_high]))

    hidden = jax.nn.silu(pre.astype(F32)).astype(BF16)
    hidden_far = jax.nn.silu(pre_partner.astype(F32)).astype(BF16)

    def ordered(replica0, replica1):
        return jnp.concatenate([pick(near, replica0, replica1), pick(near, replica1, replica0)], 1)

    h_low, h_high = ordered(hidden[0], hidden_far[1]), ordered(hidden_far[0], hidden[1])
    h_pairs = jnp.stack([pick(even, h_low, h_high), pick(even, h_high, h_low)])
    g_here = pick(outer, grads[0], grads[2])
    g_across = swap(pick(outer, grads[2], grads[0]), 2)
    g_sibling = swap(pick(outer, grads[1], grads[3]), 1)
    g_partner = swap(pick(outer, grads[3], grads[1]), 3)
    grad_down = down_grads(mask_d, core[None], h_pairs, g_here, g_across, g_sibling, g_partner)
    return (all_grads, grad_up, grad_down)


def solution(mesh):
    return jax.shard_map(
        per_device,
        mesh=mesh,
        in_specs=(
            P(None, None, "tp"),
            P(None, "segment", None, "tp"),
            P(None, "segment", None, "tp"),
            P(None, "segment", None, "tp"),
            P(None, "segment", "tp", None),
            P(None, "segment", None, "tp"),
            P(None, "segment", "tp", None),
        ),
        out_specs=(
            P(None, "segment", None, "tp"),
            P(None, "segment", None, "tp"),
            P(None, "segment", "tp", None),
        ),
        check_vma=False,
    )
```

profile of v0, /device:TPU:8, one launch (start us, length us, event | category | flops | bytes accessed | tf_op | source)
XLA Modules:
  0.0 322.2 jit_solution(14881023727645673311)
XLA Ops:
  8.8 13.7 %all-to-all-start = ((bf16[64,32,128]{2,1,0:T(8,128)(2,1)}), bf16[64,32,128]{2,1,0:T(8,128)(2,1)S(1)}, u32[]{:S(2)}, u32[]{:S(2)}) async-start(bf16[64,32,128]{2,1,0:T(8,128)(2,1)} %broadcast_in_dim.17), calls=%async_computation | async-start | bytes 1048576 | tf_op jit(solution)/shard_map/all_to_all | solution.py:22
  24.2 2.2 copy-done.1
  26.4 2.2 copy-done.3
  28.6 4.2 %prepare.2 = (bf16[256,2048]{1,0:T(8,128)(2,1)S(1)}, bf16[256,2048]{1,0:T(8,128)(2,1)}, bf16[2048,256]{1,0:T(8,128)(2,1)S(1)}, bf16[2048,256]{1,0:T(8,128)(2,1)}) custom-call(s32[3]{0:T(128)S(1)} %pad_add_fusion.info, s32[128]{0:T(128)S(1)} %reshape.142.mask_u, s32[128]{0:T(128)S(1)} %reshape.143.mask_d, bf16[2,1,4096,256]{3,2,1,0:T(8,128)(2,1)S(1)} %copy-done.1, ...), custom_call_target="tpu_custom_call" | custom-call | bytes 8388608 | tf_op jit(solution)/shard_map/prepare/pallas_call | solution.py:76
  34.4 8.1 %all-to-all-done = bf16[64,32,128]{2,1,0:T(8,128)(2,1)S(1)} async-done(((bf16[64,32,128]{2,1,0:T(8,128)(2,1)}), bf16[64,32,128]{2,1,0:T(8,128)(2,1)S(1)}, u32[]{:S(2)}, u32[]{:S(2)}) %all-to-all-start) | async-done | bytes 524320 | tf_op jit(solution)/shard_map/all_to_all | solution.py:22
  48.8 2.2 collective-permute-done.4
  52.3 2.5 up.7
  54.8 5.5 %all-to-all-start.1 = ((bf16[64,32,128]{2,1,0:T(8,128)(2,1)}), bf16[64,32,128]{2,1,0:T(8,128)(2,1)}, u32[]{:S(2)}, u32[]{:S(2)}) async-start(bf16[64,32,128]{2,1,0:T(8,128)(2,1)} %bitcast.18), calls=%async_computation.1 | async-start | bytes 1048576 | tf_op jit(solution)/shard_map/all_to_all | solution.py:22
  60.3 19.2 %all-to-all-done.1 = bf16[64,32,128]{2,1,0:T(8,128)(2,1)} async-done(((bf16[64,32,128]{2,1,0:T(8,128)(2,1)}), bf16[64,32,128]{2,1,0:T(8,128)(2,1)}, u32[]{:S(2)}, u32[]{:S(2)}) %all-to-all-start.1) | async-done | bytes 524320 | tf_op jit(solution)/shard_map/all_to_all | solution.py:22
  81.6 5.4 %all-to-all-start.2 = ((bf16[64,32,128]{2,1,0:T(8,128)(2,1)}), bf16[64,32,128]{2,1,0:T(8,128)(2,1)S(1)}, u32[]{:S(2)}, u32[]{:S(2)}) async-start(bf16[64,32,128]{2,1,0:T(8,128)(2,1)} %broadcast_in_dim.39), calls=%async_computation.2 | async-start | bytes 1048576 | tf_op jit(solution)/shard_map/all_to_all | solution.py:22
  86.9 19.0 %all-to-all-done.2 = bf16[64,32,128]{2,1,0:T(8,128)(2,1)S(1)} async-done(((bf16[64,32,128]{2,1,0:T(8,128)(2,1)}), bf16[64,32,128]{2,1,0:T(8,128)(2,1)S(1)}, u32[]{:S(2)}, u32[]{:S(2)}) %all-to-all-start.2) | async-done | bytes 524320 | tf_op jit(solution)/shard_map/all_to_all | solution.py:22
  109.9 5.2 %all-to-all-start.3 = ((bf16[64,32,128]{2,1,0:T(8,128)(2,1)}), bf16[64,32,128]{2,1,0:T(8,128)(2,1)S(1)}, u32[]{:S(2)}, u32[]{:S(2)}) async-start(bf16[64,32,128]{2,1,0:T(8,128)(2,1)} %bitcast.20), calls=%async_computation.3 | async-start | bytes 1048576 | tf_op jit(solution)/shard_map/all_to_all | solution.py:22
  115.2 2.2 copy-done.2
  117.4 2.2 copy-done.4
  119.6 3.9 %prepare.3 = (bf16[256,2048]{1,0:T(8,128)(2,1)S(1)}, bf16[256,2048]{1,0:T(8,128)(2,1)}, bf16[2048,256]{1,0:T(8,128)(2,1)S(1)}, bf16[2048,256]{1,0:T(8,128)(2,1)S(1)}) custom-call(s32[3]{0:T(128)S(1)} %pad_add_fusion.1.info, s32[128]{0:T(128)S(1)} %reshape.142.mask_u, s32[128]{0:T(128)S(1)} %reshape.143.mask_d, bf16[2,1,4096,256]{3,2,1,0:T(8,128)(2,1)S(1)} %copy-done.2, ...), custom_call_target="tpu_custom_call" | custom-call | bytes 8388608 | tf_op jit(solution)/shard_map/prepare/pallas_call | solution.py:76
  126.5 9.1 %all-to-all-done.3 = bf16[64,32,128]{2,1,0:T(8,128)(2,1)S(1)} async-done(((bf16[64,32,128]{2,1,0:T(8,128)(2,1)}), bf16[64,32,128]{2,1,0:T(8,128)(2,1)S(1)}, u32[]{:S(2)}, u32[]{:S(2)}) %all-to-all-start.3) | async-done | bytes 524320 | tf_op jit(solution)/shard_map/all_to_all | solution.py:22
  136.6 6.3 %all-to-all-start.4 = ((bf16[64,32,128]{2,1,0:T(8,128)(2,1)}), bf16[64,32,128]{2,1,0:T(8,128)(2,1)S(1)}, u32[]{:S(2)}, u32[]{:S(2)}) async-start(bf16[64,32,128]{2,1,0:T(8,128)(2,1)} %broadcast_in_dim.40), calls=%async_computation.4 | async-start | bytes 1048576 | tf_op jit(solution)/shard_map/all_to_all | solution.py:22
  144.3 1.8 collective-permute-start.17
  146.1 17.0 %all-to-all-done.4 = bf16[64,32,128]{2,1,0:T(8,128)(2,1)S(1)} async-done(((bf16[64,32,128]{2,1,0:T(8,128)(2,1)}), bf16[64,32,128]{2,1,0:T(8,128)(2,1)S(1)}, u32[]{:S(2)}, u32[]{:S(2)}) %all-to-all-start.4) | async-done | bytes 524320 | tf_op jit(solution)/shard_map/all_to_all | solution.py:22
  167.1 5.3 %all-to-all-start.5 = ((bf16[64,32,128]{2,1,0:T(8,128)(2,1)}), bf16[64,32,128]{2,1,0:T(8,128)(2,1)S(1)}, u32[]{:S(2)}, u32[]{:S(2)}) async-start(bf16[64,32,128]{2,1,0:T(8,128)(2,1)} %bitcast.26), calls=%async_computation.5 | async-start | bytes 1048576 | tf_op jit(solution)/shard_map/all_to_all | solution.py:22
  174.9 17.5 %all-to-all-done.5 = bf16[64,32,128]{2,1,0:T(8,128)(2,1)S(1)} async-done(((bf16[64,32,128]{2,1,0:T(8,128)(2,1)}), bf16[64,32,128]{2,1,0:T(8,128)(2,1)S(1)}, u32[]{:S(2)}, u32[]{:S(2)}) %all-to-all-start.5) | async-done | bytes 524320 | tf_op jit(solution)/shard_map/all_to_all | solution.py:22
  193.3 6.6 %all-to-all-start.6 = ((bf16[64,32,128]{2,1,0:T(8,128)(2,1)}), bf16[64,32,128]{2,1,0:T(8,128)(2,1)S(1)}, u32[]{:S(2)}, u32[]{:S(2)}) async-start(bf16[64,32,128]{2,1,0:T(8,128)(2,1)} %broadcast_in_dim.41), calls=%async_computation.6 | async-start | bytes 1048576 | tf_op jit(solution)/shard_map/all_to_all | solution.py:22
  205.9 14.8 %all-to-all-done.6 = bf16[64,32,128]{2,1,0:T(8,128)(2,1)S(1)} async-done(((bf16[64,32,128]{2,1,0:T(8,128)(2,1)}), bf16[64,32,128]{2,1,0:T(8,128)(2,1)S(1)}, u32[]{:S(2)}, u32[]{:S(2)}) %all-to-all-start.6) | async-done | bytes 524320 | tf_op jit(solution)/shard_map/all_to_all | solution.py:22
  220.7 1.8 down.11.part
  224.0 2.5 up.11
  226.5 5.4 %all-to-all-start.7 = ((bf16[64,32,128]{2,1,0:T(8,128)(2,1)}), bf16[64,32,128]{2,1,0:T(8,128)(2,1)S(1)}, u32[]{:S(2)}, u32[]{:S(2)}) async-start(bf16[64,32,128]{2,1,0:T(8,128)(2,1)} %bitcast.30), calls=%async_computation.7 | async-start | bytes 1048576 | tf_op jit(solution)/shard_map/all_to_all | solution.py:22
  232.9 1.9 collective-permute-start.19
  234.9 2.7 collective-permute-done.19
  238.7 61.9 %all-gather.2.cloned.1.call-done.x = bf16[2,4096,128]{2,1,0:T(8,128)(2,1)} async-done(((bf16[2,64,128]{2,1,0:T(8,128)(2,1)}), bf16[2,4096,128]{2,1,0:T(8,128)(2,1)}) %all-gather.2.cloned.1.call-update) | async-done | bytes 2097168 | tf_op jit(solution)/shard_map/all_gather | solution.py:266
  300.6 1.6 copy-done.11
  302.2 4.9 %up_grads.1 = bf16[2,1,2048,256]{3,2,1,0:T(8,128)(2,1)} custom-call(s32[128]{0:T(128)S(1)} %reshape.142.mask_u, bf16[2,4096,128]{2,1,0:T(8,128)(2,1)S(1)} %copy-done.11, bf16[2,256,256]{2,1,0:T(8,128)(2,1)S(1)} %pad_maximum_fusion.du), custom_call_target="tpu_custom_call" | custom-call | flops 536870912 | bytes 4194304 | tf_op jit(solution)/shard_map/up_grads/pallas_call | solution.py:176
  307.3 6.6 %down_grads.1 = bf16[2,1,256,2048]{3,2,1,0:T(8,128)(2,1)} custom-call(s32[128]{0:T(128)S(1)} %reshape.143.mask_d, s32[1]{0:T(128)} %bitcast.11.core, bf16[2,256,256]{2,1,0:T(8,128)(2,1)S(1)} %pad_maximum_fusion.1.h, bf16[2048,128]{1,0:T(8,128)(2,1)S(1)} %get-tuple-element.44.here, bf16[2048,128]{1,0:T(8,128)(2,1)S(1)} %collective-permute-done.21.across, ...), custom_call_target="tpu_custom_call" | custom-call | flops 536870912 | bytes 4194304 | tf_op jit(solution)/shard_map/down_grads/pallas_call | solution.py:228
  (138 shorter events, 42.4 us)
Async XLA Ops:
  8.8 33.7 %all-to-all-start = ((bf16[64,32,128]{2,1,0:T(8,128)(2,1)}), bf16[64,32,128]{2,1,0:T(8,128)(2,1)S(1)}, u32[]{:S(2)}, u32[]{:S(2)}) async-start(bf16[64,32,128]{2,1,0:T(8,128)(2,1)} %broadcast_in_dim.17), calls=%async_computation | async-start | bytes 1048576 | tf_op jit(solution)/shard_map/all_to_all | solution.py:22
  33.9 14.1 %collective-permute-start.2 = (bf16[256,2048]{1,0:T(8,128)(2,1)}, bf16[256,2048]{1,0:T(8,128)(2,1)S(1)}, u32[]{:S(2)}, u32[]{:S(2)}) collective-permute-start(bf16[256,2048]{1,0:T(8,128)(2,1)} %get-tuple-element.22), channel_id=1, source_target_pairs={{0,64},{64,0},{128,192},{192,128},{1,65},{65,1},{129,193},{193,129... | collective-permute-start | bytes 3145736 | tf_op jit(solution)/shard_map/ppermute | solution.py:18
  33.9 17.2 %collective-permute-start.1 = (bf16[2048,256]{1,0:T(8,128)(2,1)}, bf16[2048,256]{1,0:T(8,128)(2,1)}, u32[]{:S(2)}, u32[]{:S(2)}) collective-permute-start(bf16[2048,256]{1,0:T(8,128)(2,1)} %get-tuple-element.20), channel_id=1, source_target_pairs={{0,64},{64,0},{128,192},{192,128},{1,65},{65,1},{129,193},{193,129... | collective-permute-start | bytes 3145736 | tf_op jit(solution)/shard_map/ppermute | solution.py:18
  43.2 2.9 collective-permute-start
  44.0 4.9 %collective-permute-start.5 = (bf16[256,128]{1,0:T(8,128)(2,1)S(1)}, bf16[256,128]{1,0:T(8,128)(2,1)S(1)}, u32[]{:S(2)}, u32[]{:S(2)}) collective-permute-start(bf16[256,128]{1,0:T(8,128)(2,1)S(1)} %bitcast.103), channel_id=1, source_target_pairs={{0,128},{64,192},{128,0},{192,64},{1,129},{65,193},{129,1},{193,65... | collective-permute-start | bytes 196616 | tf_op jit(solution)/shard_map/ppermute | solution.py:18
  45.5 5.6 %collective-permute-start.4 = (bf16[2,256,128]{2,1,0:T(8,128)(2,1)S(1)}, bf16[2,256,128]{2,1,0:T(8,128)(2,1)S(1)}, u32[]{:S(2)}, u32[]{:S(2)}) collective-permute-start(bf16[2,256,128]{2,1,0:T(8,128)(2,1)S(1)} %bitcast.98), channel_id=1, source_target_pairs={{0,192},{64,128},{128,64},{192,0},{1,193},{65,129},{129,65},{193,1... | collective-permute-start | bytes 393224 | tf_op jit(solution)/shard_map/ppermute | solution.py:18
  48.5 2.6 collective-permute-start.3
  54.8 24.7 %all-to-all-start.1 = ((bf16[64,32,128]{2,1,0:T(8,128)(2,1)}), bf16[64,32,128]{2,1,0:T(8,128)(2,1)}, u32[]{:S(2)}, u32[]{:S(2)}) async-start(bf16[64,32,128]{2,1,0:T(8,128)(2,1)} %bitcast.18), calls=%async_computation.1 | async-start | bytes 1048576 | tf_op jit(solution)/shard_map/all_to_all | solution.py:22
  81.6 24.4 %all-to-all-start.2 = ((bf16[64,32,128]{2,1,0:T(8,128)(2,1)}), bf16[64,32,128]{2,1,0:T(8,128)(2,1)S(1)}, u32[]{:S(2)}, u32[]{:S(2)}) async-start(bf16[64,32,128]{2,1,0:T(8,128)(2,1)} %broadcast_in_dim.39), calls=%async_computation.2 | async-start | bytes 1048576 | tf_op jit(solution)/shard_map/all_to_all | solution.py:22
  106.5 1.4 collective-permute-start.6
  109.9 25.7 %all-to-all-start.3 = ((bf16[64,32,128]{2,1,0:T(8,128)(2,1)}), bf16[64,32,128]{2,1,0:T(8,128)(2,1)S(1)}, u32[]{:S(2)}, u32[]{:S(2)}) async-start(bf16[64,32,128]{2,1,0:T(8,128)(2,1)} %bitcast.20), calls=%async_computation.3 | async-start | bytes 1048576 | tf_op jit(solution)/shard_map/all_to_all | solution.py:22
  125.5 20.6 %collective-permute-start.8 = (bf16[256,2048]{1,0:T(8,128)(2,1)}, bf16[256,2048]{1,0:T(8,128)(2,1)}, u32[]{:S(2)}, u32[]{:S(2)}) collective-permute-start(bf16[256,2048]{1,0:T(8,128)(2,1)} %get-tuple-element.28), channel_id=1, source_target_pairs={{0,64},{64,0},{128,192},{192,128},{1,65},{65,1},{129,193},{193,129... | collective-permute-start | bytes 3145736 | tf_op jit(solution)/shard_map/ppermute | solution.py:18
  136.6 26.6 %all-to-all-start.4 = ((bf16[64,32,128]{2,1,0:T(8,128)(2,1)}), bf16[64,32,128]{2,1,0:T(8,128)(2,1)S(1)}, u32[]{:S(2)}, u32[]{:S(2)}) async-start(bf16[64,32,128]{2,1,0:T(8,128)(2,1)} %broadcast_in_dim.40), calls=%async_computation.4 | async-start | bytes 1048576 | tf_op jit(solution)/shard_map/all_to_all | solution.py:22
  142.9 20.9 %collective-permute-start.7 = (bf16[2048,256]{1,0:T(8,128)(2,1)}, bf16[2048,256]{1,0:T(8,128)(2,1)}, u32[]{:S(2)}, u32[]{:S(2)}) collective-permute-start(bf16[2048,256]{1,0:T(8,128)(2,1)} %copy-done.16), channel_id=1, source_target_pairs={{0,64},{64,0},{128,192},{192,128},{1,65},{65,1},{129,193},{193,129... | collective-permute-start | bytes 3145736 | tf_op jit(solution)/shard_map/ppermute | solution.py:18
  143.1 20.7 %collective-permute-start.10 = (bf16[256,128]{1,0:T(8,128)(2,1)S(1)}, bf16[256,128]{1,0:T(8,128)(2,1)S(1)}, u32[]{:S(2)}, u32[]{:S(2)}) collective-permute-start(bf16[256,128]{1,0:T(8,128)(2,1)S(1)} %bitcast.99), channel_id=1, source_target_pairs={{0,64},{64,0},{128,192},{192,128},{1,65},{65,1},{129,193},{193,129... | collective-permute-start | bytes 196616 | tf_op jit(solution)/shard_map/ppermute | solution.py:18
  144.3 28.2 %collective-permute-start.17 = (bf16[64,128]{1,0:T(8,128)(2,1)}, bf16[64,128]{1,0:T(8,128)(2,1)}, u32[]{:S(2)}, u32[]{:S(2)}) collective-permute-start(bf16[64,128]{1,0:T(8,128)(2,1)} %get-tuple-element.65), channel_id=1, source_target_pairs={{0,192},{64,128},{128,64},{192,0},{1,193},{65,129},{129,65},{193,1... | collective-permute-start | bytes 49160 | tf_op jit(solution)/shard_map/ppermute | solution.py:18
  146.1 26.4 %collective-permute-start.18 = (bf16[64,128]{1,0:T(8,128)(2,1)}, bf16[64,128]{1,0:T(8,128)(2,1)}, u32[]{:S(2)}, u32[]{:S(2)}) collective-permute-start(bf16[64,128]{1,0:T(8,128)(2,1)} %get-tuple-element.66), channel_id=1, source_target_pairs={{0,192},{64,128},{128,64},{192,0},{1,193},{65,129},{129,65},{193,1... | collective-permute-start | bytes 49160 | tf_op jit(solution)/shard_map/ppermute | solution.py:18
  163.7 1.4 collective-permute-start.9
  167.1 25.2 %all-to-all-start.5 = ((bf16[64,32,128]{2,1,0:T(8,128)(2,1)}), bf16[64,32,128]{2,1,0:T(8,128)(2,1)S(1)}, u32[]{:S(2)}, u32[]{:S(2)}) async-start(bf16[64,32,128]{2,1,0:T(8,128)(2,1)} %bitcast.26), calls=%async_computation.5 | async-start | bytes 1048576 | tf_op jit(solution)/shard_map/all_to_all | solution.py:22
  172.4 128.2 %all-gather.2.cloned.1.call-start = ((), (), s32[]{:S(2)}) async-start(), calls=%async_computation.8 | async-start | bytes 2129920 | tf_op jit(solution)/shard_map/all_gather | solution.py:266
  193.3 27.3 %all-to-all-start.6 = ((bf16[64,32,128]{2,1,0:T(8,128)(2,1)}), bf16[64,32,128]{2,1,0:T(8,128)(2,1)S(1)}, u32[]{:S(2)}, u32[]{:S(2)}) async-start(bf16[64,32,128]{2,1,0:T(8,128)(2,1)} %broadcast_in_dim.41), calls=%async_computation.6 | async-start | bytes 1048576 | tf_op jit(solution)/shard_map/all_to_all | solution.py:22
  200.9 21.5 %collective-permute-start.15 = (bf16[64,128]{1,0:T(8,128)(2,1)S(1)}, bf16[64,128]{1,0:T(8,128)(2,1)}, u32[]{:S(2)}, u32[]{:S(2)}) collective-permute-start(bf16[64,128]{1,0:T(8,128)(2,1)S(1)} %constant_dynamic-slice_fusion), channel_id=1, source_target_pairs={{0,64},{64,0},{128,192},{192,128},{1,65},{65,1},{129,193},{193,129... | collective-permute-start | bytes 49160 | tf_op jit(solution)/shard_map/ppermute | solution.py:18
  202.5 32.3 %collective-permute-start.20 = (bf16[256,128]{1,0:T(8,128)(2,1)}, bf16[256,128]{1,0:T(8,128)(2,1)}, u32[]{:S(2)}, u32[]{:S(2)}) collective-permute-start(bf16[256,128]{1,0:T(8,128)(2,1)} %broadcast_select_fusion.18), channel_id=1, source_target_pairs={{0,192},{64,128},{128,64},{192,0},{1,193},{65,129},{129,65},{193,1... | collective-permute-start | bytes 196616 | tf_op jit(solution)/shard_map/ppermute | solution.py:18
  204.1 18.5 %collective-permute-start.14 = (bf16[64,128]{1,0:T(8,128)(2,1)S(1)}, bf16[64,128]{1,0:T(8,128)(2,1)}, u32[]{:S(2)}, u32[]{:S(2)}) collective-permute-start(bf16[64,128]{1,0:T(8,128)(2,1)S(1)} %constant_dynamic-slice_fusion.1), channel_id=1, source_target_pairs={{0,64},{64,0},{128,192},{192,128},{1,65},{65,1},{129,193},{193,129... | collective-permute-start | bytes 49160 | tf_op jit(solution)/shard_map/ppermute | solution.py:18
  205.2 102.0 %collective-permute-start.22 = (bf16[2048,128]{1,0:T(8,128)(2,1)}, bf16[2048,128]{1,0:T(8,128)(2,1)S(1)}, u32[]{:S(2)}, u32[]{:S(2)}) collective-permute-start(bf16[2048,128]{1,0:T(8,128)(2,1)} %get-tuple-element.42), channel_id=1, source_target_pairs={{0,64},{64,0},{128,192},{192,128},{1,65},{65,1},{129,193},{193,129... | collective-permute-start | bytes 1572872 | tf_op jit(solution)/shard_map/ppermute | solution.py:18
  205.7 101.5 %collective-permute-start.23 = (bf16[2048,128]{1,0:T(8,128)(2,1)}, bf16[2048,128]{1,0:T(8,128)(2,1)}, u32[]{:S(2)}, u32[]{:S(2)}) collective-permute-start(bf16[2048,128]{1,0:T(8,128)(2,1)} %get-tuple-element.41), channel_id=1, source_target_pairs={{0,192},{64,128},{128,64},{192,0},{1,193},{65,129},{129,65},{193,1... | collective-permute-start | bytes 1572872 | tf_op jit(solution)/shard_map/ppermute | solution.py:18
  222.6 91.3 %collective-permute-start.16 = (bf16[64,128]{1,0:T(8,128)(2,1)S(1)}, bf16[64,128]{1,0:T(8,128)(2,1)}, u32[]{:S(2)}, u32[]{:S(2)}) collective-permute-start(bf16[64,128]{1,0:T(8,128)(2,1)S(1)} %select_select_fusion), channel_id=1, source_target_pairs={{0,128},{64,192},{128,0},{192,64},{1,129},{65,193},{129,1},{193,65... | collective-permute-start | bytes 49160 | tf_op jit(solution)/shard_map/ppermute | solution.py:18
  223.9 9.0 %collective-permute-start.11 = (bf16[64,128]{1,0:T(8,128)(2,1)S(1)}, bf16[64,128]{1,0:T(8,128)(2,1)S(1)}, u32[]{:S(2)}, u32[]{:S(2)}) collective-permute-start(bf16[64,128]{1,0:T(8,128)(2,1)S(1)} %constant_dynamic-slice_fusion.2), channel_id=1, source_target_pairs={{0,64},{64,0},{128,192},{192,128},{1,65},{65,1},{129,193},{193,129... | collective-permute-start | bytes 49160 | tf_op jit(solution)/shard_map/ppermute | solution.py:18
  226.5 80.5 %all-to-all-start.7 = ((bf16[64,32,128]{2,1,0:T(8,128)(2,1)}), bf16[64,32,128]{2,1,0:T(8,128)(2,1)S(1)}, u32[]{:S(2)}, u32[]{:S(2)}) async-start(bf16[64,32,128]{2,1,0:T(8,128)(2,1)} %bitcast.30), calls=%async_computation.7 | async-start | bytes 1048576 | tf_op jit(solution)/shard_map/all_to_all | solution.py:22
  232.9 4.8 %collective-permute-start.19 = (bf16[256,128]{1,0:T(8,128)(2,1)S(1)}, bf16[256,128]{1,0:T(8,128)(2,1)S(1)}, u32[]{:S(2)}, u32[]{:S(2)}) collective-permute-start(bf16[256,128]{1,0:T(8,128)(2,1)S(1)} %broadcast_select_fusion.19), channel_id=1, source_target_pairs={{0,192},{64,128},{128,64},{192,0},{1,193},{65,129},{129,65},{193,1... | collective-permute-start | bytes 196616 | tf_op jit(solution)/shard_map/ppermute | solution.py:18
  234.8 72.4 %collective-permute-start.21 = (bf16[2048,128]{1,0:T(8,128)(2,1)}, bf16[2048,128]{1,0:T(8,128)(2,1)S(1)}, u32[]{:S(2)}, u32[]{:S(2)}) collective-permute-start(bf16[2048,128]{1,0:T(8,128)(2,1)} %get-tuple-element.43), channel_id=1, source_target_pairs={{0,128},{64,192},{128,0},{192,64},{1,129},{65,193},{129,1},{193,65... | collective-permute-start | bytes 1572872 | tf_op jit(solution)/shard_map/ppermute | solution.py:18
  307.2 6.7 %collective-permute-start.13 = (bf16[32,128]{1,0:T(8,128)(2,1)S(1)}, bf16[32,128]{1,0:T(8,128)(2,1)S(1)}, u32[]{:S(2)}, u32[]{:S(2)}) collective-permute-start(bf16[32,128]{1,0:T(8,128)(2,1)S(1)} %add_convert_fusion), channel_id=1, source_target_pairs={{0,64},{64,0},{128,192},{192,128},{1,65},{65,1},{129,193},{193,129... | collective-permute-start | bytes 24584 | tf_op jit(solution)/shard_map/ppermute | solution.py:18
  (22 other events, 109.3 us)
Sparse Core Ops, SparseCore 0:
  177.4 123.1 all-gather.1
where the time goes:
time: 326 us; the launch traced here: 322 us
  waiting for transfers between devices  175 us (54%)
  starting transfers between devices  64.7 us (20%)
  Pallas kernels  30.6 us (9%)
  local copies, waits for them, and re-layouts  24.8 us (8%)
  between operations  14.6 us (4%)
  other arithmetic  12.1 us (4%)
    all_to_all x8, waiting for transfers between devices, exchange(): return lax.all_to_all(parts, 'tp', 0, 0, tiled=True)  105 us
    all_gather x1, waiting for transfers between devices, per_device(): x_full = lax.all_gather(x_sent, 'tp', axis=1, tiled=True)  61.9 us
    all_to_all x8, starting transfers between devices, exchange(): return lax.all_to_all(parts, 'tp', 0, 0, tiled=True)  53.3 us
    unnamed x44, local copies, waits for them, and re-layouts  18.2 us
    ppermute x24, starting transfers between devices, swap(): return lax.ppermute(value, 'segment', [(s, s ^ bits) for s in range(4)])  11.4 us
    ppermute x24, waiting for transfers between devices, swap(): return lax.ppermute(value, 'segment', [(s, s ^ bits) for s in range(4)])  8.8 us
    pallas_call x2, Pallas kernels, prepare(): pl.pallas_call(functools.partial(prepare_kernel, share), grid_spec=pltpu....  8.16 us
    pallas_call x4, Pallas kernels, up_step(): pl.pallas_call(up_kernel, in_specs=[pl.BlockSpec(memory_space=pltpu.SMEM)...  7.67 us
  transfers between devices with their start and end apart: 33, of which 13 were waited for; matrix products, arithmetic and copies ran while one was open for 5% of the time, Pallas kernels for 8%

commit v1 on v0

--- a/solution.py
+++ b/solution.py
@@ -150,12 +150,13 @@
     )(flag, keep, came, part, peer, pre)
 
 
-def up_grad_kernel(mask_u, x, du, out):
+def up_grad_kernel(mask_u, line, x, du, out):
     i = pl.program_id(0)
     rows, hidden = out.shape[2], out.shape[3]
+    tokens = x.shape[4]
     pairs = hidden // BLOCK
     steps = pl.num_programs(0)
-    both = jnp.concatenate([x[0], x[1]], axis=1)
+    both = jnp.concatenate([x[:, 0, 0].reshape(rows, tokens), x[:, 1, 0].reshape(rows, tokens)], axis=1)
     total = lax.dot_general(both, du[0], NT, preferred_element_type=F32)
     layer = i // (steps // 2)
     blocks = steps * rows // BLOCK
@@ -167,28 +168,58 @@
             out[0, 0, at_rows, lanes] = kept_blocks(total[at_rows, lanes], mask_u[(layer * blocks + block) * pairs + h]).astype(BF16)
 
 
-def up_grads(mask_u, x, du):
-    _, features, tokens = x.shape
+def up_grads(mask_u, line, x, du):
+    inner, _, planes, width, tokens = x.shape
+    features = inner * planes * width
     hidden = du.shape[1]
     half = features // 2
-    rows = min(512, half)
+    rows = min(512, inner * width)
     per = half // rows
+    plane = inner * width // rows
     return pl.pallas_call(
         up_grad_kernel,
         grid_spec=pltpu.PrefetchScalarGridSpec(
-            num_scalar_prefetch=1,
+            num_scalar_prefetch=2,
             grid=(2 * per,),
             in_specs=[
-                pl.BlockSpec((2, rows, tokens), lambda i, _: (0, i, 0)),
-                pl.BlockSpec((1, hidden, 2 * tokens), lambda i, _: (i // per, 0, 0)),
+                pl.BlockSpec(
+                    (rows // width, 2, 1, width, tokens), lambda i, _, line: (i % plane, 0, (i // plane) ^ line[0], 0, 0)
+                ),
+                pl.BlockSpec((1, hidden, 2 * tokens), lambda i, *_: (i // per, 0, 0)),
             ],
-            out_specs=pl.BlockSpec((1, 1, rows, hidden), lambda i, _: (i // per, 0, i % per, 0)),
+            out_specs=pl.BlockSpec((1, 1, rows, hidden), lambda i, *_: (i // per, 0, i % per, 0)),
         ),
         out_shape=jax.ShapeDtypeStruct((2, 1, half, hidden), BF16),
         compiler_params=params(),
         cost_estimate=pl.CostEstimate(flops=4 * features * hidden * tokens, bytes_accessed=4 * features * hidden, transcendentals=0),
         name="up_grads",
-    )(mask_u, x, du)
+    )(mask_u, line, x, du)
+
+
+def fold_kernel(place, landed, grad, out):
+    members, share, _ = landed.shape
+    own = grad[pl.ds(pl.multiple_of(place[0] * share, share), share), :].astype(F32)
+    total = lax.fori_loop(0, members, lambda j, acc: acc + landed[j].astype(F32), jnp.zeros(own.shape, F32), unroll=8)
+    result = (own + total).astype(BF16)
+
+    def put(j, carry):
+        out[j] = result
+        return carry
+
+    lax.fori_loop(0, members, put, 0, unroll=8)
+
+
+def fold(place, landed, grad):
+    vmem = pl.BlockSpec(memory_space=pltpu.VMEM)
+    return pl.pallas_call(
+        fold_kernel,
+        in_specs=[pl.BlockSpec(memory_space=pltpu.SMEM), vmem, vmem],
+        out_specs=vmem,
+        out_shape=jax.ShapeDtypeStruct(landed.shape, BF16),
+        compiler_params=params(),
+        cost_estimate=pl.CostEstimate(flops=landed.size, bytes_accessed=4 * landed.size, transcendentals=0),
+        name="fold",
+    )(place, landed, grad)
 
 
 def down_grad_kernel(mask_d, core, h, here, across, sibling, partner, out):
@@ -263,7 +294,11 @@
     x_far0, x_far1 = swap(xs[0], 3), swap(xs[1], 3)
     low_member = place < members // 2
     x_sent = jnp.stack([pick(low_member, xs[0], x_far0), pick(low_member, x_far1, xs[1])])
-    x_full = lax.all_gather(x_sent, "tp", axis=1, tiled=True)
+    inner = max(1, members // 4)
+    planes = members // inner
+    lines = [x_sent] + [lax.ppermute(x_sent, "tp", [(i, i ^ (k * inner)) for i in range(members)]) for k in range(1, planes)]
+    groups = [[p * inner + q for q in range(inner)] for p in range(planes)]
+    x_full = lax.all_gather(jnp.stack(lines, 1), "tp", axis_index_groups=groups)
 
     pre = saved_pre[:, 0].transpose(0, 2, 1)
     pre_partner = swap(pre, 3)
@@ -304,16 +339,13 @@
         partial = down_step(flag, keep_d, came_d, grad)
         dus[layer], out = up_step(flag, keep_u, came_u, partial, swap(partial, 1), pre_of[layer])
         landed = exchange(out.reshape(members, share, tokens))
-        total = jnp.sum(landed.astype(F32), axis=0)
         if layer:
-            own = lax.dynamic_slice_in_dim(grad, place * share, share, 0)
-            out = (own.astype(F32) + total).astype(BF16)
-            grad = exchange(jnp.broadcast_to(out[None], (members, share, tokens))).reshape(half, tokens)
+            grad = exchange(fold(place[None], landed, grad)).reshape(half, tokens)
             mine = lax.dynamic_slice_in_dim(grad, (place % (members // 2)) * 2 * share, 2 * share, 0)
             shards[layer] = pick(place // (members // 2) == core, mine, swap(mine, 1))
         else:
             own = lax.dynamic_slice_in_dim(shards[1], core * share, share, 0)
-            out = (own.astype(F32) + total).astype(BF16)
+            out = (own.astype(F32) + jnp.sum(landed.astype(F32), axis=0)).astype(BF16)
             peer = swap(out, 1)
             shards[0] = pick(even, jnp.concatenate([out, peer]), jnp.concatenate([peer, out]))
 
@@ -328,7 +360,7 @@
     high_own, high_far = pick(near, first_du, second_du), pick(near, far_first, far_second)
     du_low = jnp.concatenate([pick(near, low_own, low_far), pick(near, low_far, low_own)], 1)
     du_high = jnp.concatenate([pick(near, high_own, high_far), pick(near, high_far, high_own)], 1)
-    grad_up = up_grads(mask_u, x_full, jnp.stack([du_low, du_high]))
+    grad_up = up_grads(mask_u, (place // inner)[None], x_full, jnp.stack([du_low, du_high]))
 
     hidden = jax.nn.silu(pre.astype(F32)).astype(BF16)
     hidden_far = jax.nn.silu(pre_partner.astype(F32)).astype(BF16)

time: 326 us -> 284 us (0.87)
  waiting for transfers between devices: 175 us -> 123 us
  starting transfers between devices: 64.7 us -> 72.7 us
    all_gather x1, waiting for transfers between devices: 61.9 us -> 0.01 us  [per_device(): x_full = lax.all_gather(jnp.stack(lines, 1), 'tp', axis_index_groups=groups)]
    all_to_all x8, waiting for transfers between devices: 105 us -> 110 us  [exchange(): return lax.all_to_all(parts, 'tp', 0, 0, tiled=True)]
    ppermute x24, waiting for transfers between devices: 8.8 us -> 13.7 us  [swap(): return lax.ppermute(value, 'segment', [(s, s ^ bits) for s in range(4)])]
    ppermute x0 -> x3, starting transfers between devices: none -> 4.18 us  [per_device(): lax.ppermute(x_sent, 'tp', [(i, i ^ k * inner) for i in range(members)])]
    unnamed x44 -> x60, local copies, waits for them, and re-layouts: 18.2 us -> 21.2 us
  transfers between devices with their start and end apart: 33 -> 36, of which waited for: 13 -> 16; matrix products, arithmetic and copies ran while one was open for 5% -> 6% of each run, Pallas kernels for 8% -> 11%
where the time goes in v1:
time: 284 us; the launch traced here: 282 us
  waiting for transfers between devices  123 us (43%)
  starting transfers between devices  72.7 us (26%)
  Pallas kernels  32.6 us (11%)
  local copies, waits for them, and re-layouts  26.4 us (9%)
  between operations  14.7 us (5%)
  other arithmetic  11.7 us (4%)
    all_to_all x8, waiting for transfers between devices, exchange(): return lax.all_to_all(parts, 'tp', 0, 0, tiled=True)  110 us
    all_to_all x8, starting transfers between devices, exchange(): return lax.all_to_all(parts, 'tp', 0, 0, tiled=True)  55.7 us
    unnamed x60, local copies, waits for them, and re-layouts  21.2 us
    ppermute x24, waiting for transfers between devices, swap(): return lax.ppermute(value, 'segment', [(s, s ^ bits) for s in range(4)])  13.7 us
    ppermute x24, starting transfers between devices, swap(): return lax.ppermute(value, 'segment', [(s, s ^ bits) for s in range(4)])  12.8 us
    pallas_call x2, Pallas kernels, prepare(): pl.pallas_call(functools.partial(prepare_kernel, share), grid_spec=pltpu....  8.2 us
    select_n x12, other arithmetic, pick(): return jnp.where(condition, a, b)  8.02 us
    pallas_call x1, Pallas kernels, down_grads(): pl.pallas_call(down_grad_kernel, grid_spec=pltpu.PrefetchScalarGridSpec(n...  7.19 us
  transfers between devices with their start and end apart: 36, of which 16 were waited for; matrix products, arithmetic and copies ran while one was open for 6% of the time, Pallas kernels for 11%

profile of v1, /device:TPU:8, one launch (start us, length us, event | category | flops | bytes accessed | tf_op | source)
XLA Modules:
  0.0 281.5 jit_solution(16041730679843811327)
XLA Ops:
  8.8 13.7 %all-to-all-start = ((bf16[64,32,128]{2,1,0:T(8,128)(2,1)}), bf16[64,32,128]{2,1,0:T(8,128)(2,1)S(1)}, u32[]{:S(2)}, u32[]{:S(2)}) async-start(bf16[64,32,128]{2,1,0:T(8,128)(2,1)} %broadcast_in_dim.29), calls=%async_computation | async-start | bytes 1048576 | tf_op jit(solution)/shard_map/all_to_all | solution.py:22
  24.2 2.2 copy-done.1
  26.4 2.2 copy-done.3
  28.6 4.2 %prepare.3 = (bf16[256,2048]{1,0:T(8,128)(2,1)S(1)}, bf16[256,2048]{1,0:T(8,128)(2,1)}, bf16[2048,256]{1,0:T(8,128)(2,1)S(1)}, bf16[2048,256]{1,0:T(8,128)(2,1)}) custom-call(s32[3]{0:T(128)S(1)} %pad_add_fusion.1.info, s32[128]{0:T(128)S(1)} %reshape.137.mask_u, s32[128]{0:T(128)S(1)} %reshape.138.mask_d, bf16[2,1,4096,256]{3,2,1,0:T(8,128)(2,1)S(1)} %copy-done.1, ...), custom_call_target="tpu_custom_call" | custom-call | bytes 8388608 | tf_op jit(solution)/shard_map/prepare/pallas_call | solution.py:76
  34.4 8.1 %all-to-all-done = bf16[64,32,128]{2,1,0:T(8,128)(2,1)S(1)} async-done(((bf16[64,32,128]{2,1,0:T(8,128)(2,1)}), bf16[64,32,128]{2,1,0:T(8,128)(2,1)S(1)}, u32[]{:S(2)}, u32[]{:S(2)}) %all-to-all-start) | async-done | bytes 524320 | tf_op jit(solution)/shard_map/all_to_all | solution.py:22
  48.3 2.3 collective-permute-done.6
  55.3 5.2 %all-to-all-start.1 = ((bf16[64,32,128]{2,1,0:T(8,128)(2,1)}), bf16[64,32,128]{2,1,0:T(8,128)(2,1)S(1)}, u32[]{:S(2)}, u32[]{:S(2)}) async-start(bf16[64,32,128]{2,1,0:T(8,128)(2,1)} %bitcast.103), calls=%async_computation.1 | async-start | bytes 1048576 | tf_op jit(solution)/shard_map/all_to_all | solution.py:22
  60.5 19.1 %all-to-all-done.1.landed = bf16[64,32,128]{2,1,0:T(8,128)(2,1)S(1)} async-done(((bf16[64,32,128]{2,1,0:T(8,128)(2,1)}), bf16[64,32,128]{2,1,0:T(8,128)(2,1)S(1)}, u32[]{:S(2)}, u32[]{:S(2)}) %all-to-all-start.1) | async-done | bytes 524320 | tf_op jit(solution)/shard_map/all_to_all | solution.py:22
  80.6 5.4 %all-to-all-start.2 = ((bf16[64,32,128]{2,1,0:T(8,128)(2,1)}), bf16[64,32,128]{2,1,0:T(8,128)(2,1)S(1)}, u32[]{:S(2)}, u32[]{:S(2)}) async-start(bf16[64,32,128]{2,1,0:T(8,128)(2,1)} %fold.3), calls=%async_computation.2 | async-start | bytes 1048576 | tf_op jit(solution)/shard_map/all_to_all | solution.py:22
  86.0 2.0 collective-permute-start.17
  91.2 2.9 %collective-permute-start.21 = (bf16[2,64,128]{2,1,0:T(8,128)(2,1)S(1)}, bf16[2,64,128]{2,1,0:T(8,128)(2,1)S(1)}, u32[]{:S(2)}, u32[]{:S(2)}) collective-permute-start(bf16[2,64,128]{2,1,0:T(8,128)(2,1)S(1)} %get-tuple-element.64), channel_id=1, source_target_pairs={{0,48},{1,49},{2,50},{3,51},{4,52},{5,53},{6,54},{7,55},{8,56},{9,... | collective-permute-start | bytes 98312 | tf_op jit(solution)/shard_map/ppermute | solution.py:299
  95.4 9.4 %all-to-all-done.2 = bf16[64,32,128]{2,1,0:T(8,128)(2,1)S(1)} async-done(((bf16[64,32,128]{2,1,0:T(8,128)(2,1)}), bf16[64,32,128]{2,1,0:T(8,128)(2,1)S(1)}, u32[]{:S(2)}, u32[]{:S(2)}) %all-to-all-start.2) | async-done | bytes 524320 | tf_op jit(solution)/shard_map/all_to_all | solution.py:22
  109.6 5.2 %all-to-all-start.3 = ((bf16[64,32,128]{2,1,0:T(8,128)(2,1)}), bf16[64,32,128]{2,1,0:T(8,128)(2,1)S(1)}, u32[]{:S(2)}, u32[]{:S(2)}) async-start(bf16[64,32,128]{2,1,0:T(8,128)(2,1)} %bitcast.22), calls=%async_computation.3 | async-start | bytes 1048576 | tf_op jit(solution)/shard_map/all_to_all | solution.py:22
  114.9 2.3 copy-done.2
  117.2 2.2 copy-done.4
  119.4 4.0 %prepare.2 = (bf16[256,2048]{1,0:T(8,128)(2,1)S(1)}, bf16[256,2048]{1,0:T(8,128)(2,1)}, bf16[2048,256]{1,0:T(8,128)(2,1)S(1)}, bf16[2048,256]{1,0:T(8,128)(2,1)S(1)}) custom-call(s32[3]{0:T(128)S(1)} %pad_add_fusion.info, s32[128]{0:T(128)S(1)} %reshape.137.mask_u, s32[128]{0:T(128)S(1)} %reshape.138.mask_d, bf16[2,1,4096,256]{3,2,1,0:T(8,128)(2,1)S(1)} %copy-done.2, ...), custom_call_target="tpu_custom_call" | custom-call | bytes 8388608 | tf_op jit(solution)/shard_map/prepare/pallas_call | solution.py:76
  126.1 11.5 %all-to-all-done.3.landed = bf16[64,32,128]{2,1,0:T(8,128)(2,1)S(1)} async-done(((bf16[64,32,128]{2,1,0:T(8,128)(2,1)}), bf16[64,32,128]{2,1,0:T(8,128)(2,1)S(1)}, u32[]{:S(2)}, u32[]{:S(2)}) %all-to-all-start.3) | async-done | bytes 524320 | tf_op jit(solution)/shard_map/all_to_all | solution.py:22
  138.4 6.6 %all-to-all-start.4 = ((bf16[64,32,128]{2,1,0:T(8,128)(2,1)}), bf16[64,32,128]{2,1,0:T(8,128)(2,1)S(1)}, u32[]{:S(2)}, u32[]{:S(2)}) async-start(bf16[64,32,128]{2,1,0:T(8,128)(2,1)} %copy-done.16), calls=%async_computation.4 | async-start | bytes 1048576 | tf_op jit(solution)/shard_map/all_to_all | solution.py:22
  145.9 18.9 %all-to-all-done.4 = bf16[64,32,128]{2,1,0:T(8,128)(2,1)S(1)} async-done(((bf16[64,32,128]{2,1,0:T(8,128)(2,1)}), bf16[64,32,128]{2,1,0:T(8,128)(2,1)S(1)}, u32[]{:S(2)}, u32[]{:S(2)}) %all-to-all-start.4) | async-done | bytes 524320 | tf_op jit(solution)/shard_map/all_to_all | solution.py:22
  168.8 6.7 %all-to-all-start.5 = ((bf16[64,32,128]{2,1,0:T(8,128)(2,1)}), bf16[64,32,128]{2,1,0:T(8,128)(2,1)S(1)}, u32[]{:S(2)}, u32[]{:S(2)}) async-start(bf16[64,32,128]{2,1,0:T(8,128)(2,1)} %bitcast.27), calls=%async_computation.5 | async-start | bytes 1048576 | tf_op jit(solution)/shard_map/all_to_all | solution.py:22
  175.8 23.1 %all-to-all-done.5.landed = bf16[64,32,128]{2,1,0:T(8,128)(2,1)S(1)} async-done(((bf16[64,32,128]{2,1,0:T(8,128)(2,1)}), bf16[64,32,128]{2,1,0:T(8,128)(2,1)S(1)}, u32[]{:S(2)}, u32[]{:S(2)}) %all-to-all-start.5) | async-done | bytes 524320 | tf_op jit(solution)/shard_map/all_to_all | solution.py:22
  199.9 7.2 %all-to-all-start.6 = ((bf16[64,32,128]{2,1,0:T(8,128)(2,1)}), bf16[64,32,128]{2,1,0:T(8,128)(2,1)}, u32[]{:S(2)}, u32[]{:S(2)}) async-start(bf16[64,32,128]{2,1,0:T(8,128)(2,1)} %fold.5), calls=%async_computation.6 | async-start | bytes 1048576 | tf_op jit(solution)/shard_map/all_to_all | solution.py:22
  211.3 2.1 broadcast_select_fusion
  214.2 13.2 %all-to-all-done.6 = bf16[64,32,128]{2,1,0:T(8,128)(2,1)} async-done(((bf16[64,32,128]{2,1,0:T(8,128)(2,1)}), bf16[64,32,128]{2,1,0:T(8,128)(2,1)}, u32[]{:S(2)}, u32[]{:S(2)}) %all-to-all-start.6) | async-done | bytes 524320 | tf_op jit(solution)/shard_map/all_to_all | solution.py:22
  234.4 2.5 up.11
  237.5 5.6 %all-to-all-start.7 = ((bf16[64,32,128]{2,1,0:T(8,128)(2,1)}), bf16[64,32,128]{2,1,0:T(8,128)(2,1)}, u32[]{:S(2)}, u32[]{:S(2)}) async-start(bf16[64,32,128]{2,1,0:T(8,128)(2,1)} %bitcast.31), calls=%async_computation.7 | async-start | bytes 1048576 | tf_op jit(solution)/shard_map/all_to_all | solution.py:22
  245.2 2.0 collective-permute-start.22
  248.0 2.1 collective-permute-done.22
  251.1 4.9 %up_grads.1 = bf16[2,1,2048,256]{3,2,1,0:T(8,128)(2,1)} custom-call(s32[128]{0:T(128)S(1)} %reshape.137.mask_u, s32[1]{0:T(128)} %bitcast.37.line, bf16[16,2,4,64,128]{4,3,2,1,0:T(8,128)(2,1)S(1)} %bitcast.100, bf16[2,256,256]{2,1,0:T(8,128)(2,1)S(1)} %pad_maximum_fusion.du), custom_call_target="tpu_custom_call" | custom-call | flops 536870912 | bytes 4194304 | tf_op jit(solution)/shard_map/up_grads/pallas_call | solution.py:179
  256.0 6.4 %all-to-all-done.7 = bf16[64,32,128]{2,1,0:T(8,128)(2,1)} async-done(((bf16[64,32,128]{2,1,0:T(8,128)(2,1)}), bf16[64,32,128]{2,1,0:T(8,128)(2,1)}, u32[]{:S(2)}, u32[]{:S(2)}) %all-to-all-start.7) | async-done | bytes 524320 | tf_op jit(solution)/shard_map/all_to_all | solution.py:22
  263.6 2.4 collective-permute-done.24.across
  266.1 7.2 %down_grads.1 = bf16[2,1,256,2048]{3,2,1,0:T(8,128)(2,1)} custom-call(s32[128]{0:T(128)S(1)} %reshape.138.mask_d, s32[1]{0:T(128)} %bitcast.3.core, bf16[2,256,256]{2,1,0:T(8,128)(2,1)S(1)} %pad_maximum_fusion.1.h, bf16[2048,128]{1,0:T(8,128)(2,1)S(1)} %get-tuple-element.44.here, bf16[2048,128]{1,0:T(8,128)(2,1)} %collective-permute-done.24.across, ...), custom_call_target="tpu_custom_call" | custom-call | flops 536870912 | bytes 4194304 | tf_op jit(solution)/shard_map/down_grads/pallas_call | solution.py:259
  (156 shorter events, 54.0 us)
Async XLA Ops:
  8.8 33.7 %all-to-all-start = ((bf16[64,32,128]{2,1,0:T(8,128)(2,1)}), bf16[64,32,128]{2,1,0:T(8,128)(2,1)S(1)}, u32[]{:S(2)}, u32[]{:S(2)}) async-start(bf16[64,32,128]{2,1,0:T(8,128)(2,1)} %broadcast_in_dim.29), calls=%async_computation | async-start | bytes 1048576 | tf_op jit(solution)/shard_map/all_to_all | solution.py:22
  33.9 11.6 %collective-permute-start.3 = (bf16[256,2048]{1,0:T(8,128)(2,1)}, bf16[256,2048]{1,0:T(8,128)(2,1)S(1)}, u32[]{:S(2)}, u32[]{:S(2)}) collective-permute-start(bf16[256,2048]{1,0:T(8,128)(2,1)} %get-tuple-element.26), channel_id=1, source_target_pairs={{0,64},{64,0},{128,192},{192,128},{1,65},{65,1},{129,193},{193,129... | collective-permute-start | bytes 3145736 | tf_op jit(solution)/shard_map/ppermute | solution.py:18
  33.9 17.7 %collective-permute-start.2 = (bf16[2048,256]{1,0:T(8,128)(2,1)}, bf16[2048,256]{1,0:T(8,128)(2,1)}, u32[]{:S(2)}, u32[]{:S(2)}) collective-permute-start(bf16[2048,256]{1,0:T(8,128)(2,1)} %get-tuple-element.24), channel_id=1, source_target_pairs={{0,64},{64,0},{128,192},{192,128},{1,65},{65,1},{129,193},{193,129... | collective-permute-start | bytes 3145736 | tf_op jit(solution)/shard_map/ppermute | solution.py:18
  43.4 4.9 %collective-permute-start.7 = (bf16[256,128]{1,0:T(8,128)(2,1)}, bf16[256,128]{1,0:T(8,128)(2,1)}, u32[]{:S(2)}, u32[]{:S(2)}) collective-permute-start(bf16[256,128]{1,0:T(8,128)(2,1)} %bitcast.19), channel_id=1, source_target_pairs={{0,128},{64,192},{128,0},{192,64},{1,129},{65,193},{129,1},{193,65... | collective-permute-start | bytes 196616 | tf_op jit(solution)/shard_map/ppermute | solution.py:18
  44.9 5.8 %collective-permute-start.6 = (bf16[2,256,128]{2,1,0:T(8,128)(2,1)S(1)}, bf16[2,256,128]{2,1,0:T(8,128)(2,1)S(1)}, u32[]{:S(2)}, u32[]{:S(2)}) collective-permute-start(bf16[2,256,128]{2,1,0:T(8,128)(2,1)S(1)} %bitcast.105), channel_id=1, source_target_pairs={{0,192},{64,128},{128,64},{192,0},{1,193},{65,129},{129,65},{193,1... | collective-permute-start | bytes 393224 | tf_op jit(solution)/shard_map/ppermute | solution.py:18
  46.0 5.5 %collective-permute-start.5 = (f32[256,128]{1,0:T(8,128)S(1)}, f32[256,128]{1,0:T(8,128)S(1)}, u32[]{:S(2)}, u32[]{:S(2)}) collective-permute-start(f32[256,128]{1,0:T(8,128)S(1)} %down.8.part), channel_id=1, source_target_pairs={{0,64},{64,0},{128,192},{192,128},{1,65},{65,1},{129,193},{193,129... | collective-permute-start | bytes 393224 | tf_op jit(solution)/shard_map/ppermute | solution.py:18
  55.3 24.4 %all-to-all-start.1 = ((bf16[64,32,128]{2,1,0:T(8,128)(2,1)}), bf16[64,32,128]{2,1,0:T(8,128)(2,1)S(1)}, u32[]{:S(2)}, u32[]{:S(2)}) async-start(bf16[64,32,128]{2,1,0:T(8,128)(2,1)} %bitcast.103), calls=%async_computation.1 | async-start | bytes 1048576 | tf_op jit(solution)/shard_map/all_to_all | solution.py:22
  80.6 24.3 %all-to-all-start.2 = ((bf16[64,32,128]{2,1,0:T(8,128)(2,1)}), bf16[64,32,128]{2,1,0:T(8,128)(2,1)S(1)}, u32[]{:S(2)}, u32[]{:S(2)}) async-start(bf16[64,32,128]{2,1,0:T(8,128)(2,1)} %fold.3), calls=%async_computation.2 | async-start | bytes 1048576 | tf_op jit(solution)/shard_map/all_to_all | solution.py:22
  86.0 123.4 %all-gather.3.cloned.1.call-start = ((), (), s32[]{:S(2)}) async-start(), calls=%async_computation.8 | async-start | bytes 2228224 | tf_op jit(solution)/shard_map/all_gather | solution.py:301
  86.0 3.4 %collective-permute-start.17 = (bf16[64,128]{1,0:T(8,128)(2,1)S(1)}, bf16[64,128]{1,0:T(8,128)(2,1)S(1)}, u32[]{:S(2)}, u32[]{:S(2)}) collective-permute-start(bf16[64,128]{1,0:T(8,128)(2,1)S(1)} %get-tuple-element.67), channel_id=1, source_target_pairs={{0,192},{64,128},{128,64},{192,0},{1,193},{65,129},{129,65},{193,1... | collective-permute-start | bytes 49160 | tf_op jit(solution)/shard_map/ppermute | solution.py:18
  88.0 3.2 %collective-permute-start.18 = (bf16[64,128]{1,0:T(8,128)(2,1)S(1)}, bf16[64,128]{1,0:T(8,128)(2,1)S(1)}, u32[]{:S(2)}, u32[]{:S(2)}) collective-permute-start(bf16[64,128]{1,0:T(8,128)(2,1)S(1)} %get-tuple-element.68), channel_id=1, source_target_pairs={{0,192},{64,128},{128,64},{192,0},{1,193},{65,129},{129,65},{193,1... | collective-permute-start | bytes 49160 | tf_op jit(solution)/shard_map/ppermute | solution.py:18
  91.2 14.3 %collective-permute-start.21 = (bf16[2,64,128]{2,1,0:T(8,128)(2,1)S(1)}, bf16[2,64,128]{2,1,0:T(8,128)(2,1)S(1)}, u32[]{:S(2)}, u32[]{:S(2)}) collective-permute-start(bf16[2,64,128]{2,1,0:T(8,128)(2,1)S(1)} %get-tuple-element.64), channel_id=1, source_target_pairs={{0,48},{1,49},{2,50},{3,51},{4,52},{5,53},{6,54},{7,55},{8,56},{9,... | collective-permute-start | bytes 98312 | tf_op jit(solution)/shard_map/ppermute | solution.py:299
  94.1 11.4 %collective-permute-start.20 = (bf16[2,64,128]{2,1,0:T(8,128)(2,1)S(1)}, bf16[2,64,128]{2,1,0:T(8,128)(2,1)S(1)}, u32[]{:S(2)}, u32[]{:S(2)}) collective-permute-start(bf16[2,64,128]{2,1,0:T(8,128)(2,1)S(1)} %get-tuple-element.64), channel_id=1, source_target_pairs={{0,32},{1,33},{2,34},{3,35},{4,36},{5,37},{6,38},{7,39},{8,40},{9,... | collective-permute-start | bytes 98312 | tf_op jit(solution)/shard_map/ppermute | solution.py:299
  94.7 10.8 %collective-permute-start.19 = (bf16[2,64,128]{2,1,0:T(8,128)(2,1)S(1)}, bf16[2,64,128]{2,1,0:T(8,128)(2,1)S(1)}, u32[]{:S(2)}, u32[]{:S(2)}) collective-permute-start(bf16[2,64,128]{2,1,0:T(8,128)(2,1)S(1)} %get-tuple-element.64), channel_id=1, source_target_pairs={{0,16},{1,17},{2,18},{3,19},{4,20},{5,21},{6,22},{7,23},{8,24},{9,... | collective-permute-start | bytes 98312 | tf_op jit(solution)/shard_map/ppermute | solution.py:299
  109.6 27.9 %all-to-all-start.3 = ((bf16[64,32,128]{2,1,0:T(8,128)(2,1)}), bf16[64,32,128]{2,1,0:T(8,128)(2,1)S(1)}, u32[]{:S(2)}, u32[]{:S(2)}) async-start(bf16[64,32,128]{2,1,0:T(8,128)(2,1)} %bitcast.22), calls=%async_computation.3 | async-start | bytes 1048576 | tf_op jit(solution)/shard_map/all_to_all | solution.py:22
  125.3 20.6 %collective-permute-start.1 = (bf16[256,2048]{1,0:T(8,128)(2,1)}, bf16[256,2048]{1,0:T(8,128)(2,1)S(1)}, u32[]{:S(2)}, u32[]{:S(2)}) collective-permute-start(bf16[256,2048]{1,0:T(8,128)(2,1)} %get-tuple-element.22), channel_id=1, source_target_pairs={{0,64},{64,0},{128,192},{192,128},{1,65},{65,1},{129,193},{193,129... | collective-permute-start | bytes 3145736 | tf_op jit(solution)/shard_map/ppermute | solution.py:18
  138.4 26.4 %all-to-all-start.4 = ((bf16[64,32,128]{2,1,0:T(8,128)(2,1)}), bf16[64,32,128]{2,1,0:T(8,128)(2,1)S(1)}, u32[]{:S(2)}, u32[]{:S(2)}) async-start(bf16[64,32,128]{2,1,0:T(8,128)(2,1)} %copy-done.16), calls=%async_computation.4 | async-start | bytes 1048576 | tf_op jit(solution)/shard_map/all_to_all | solution.py:22
  145.1 20.4 %collective-permute-start = (bf16[2048,256]{1,0:T(8,128)(2,1)}, bf16[2048,256]{1,0:T(8,128)(2,1)}, u32[]{:S(2)}, u32[]{:S(2)}) collective-permute-start(bf16[2048,256]{1,0:T(8,128)(2,1)} %copy-done.22), channel_id=1, source_target_pairs={{0,64},{64,0},{128,192},{192,128},{1,65},{65,1},{129,193},{193,129... | collective-permute-start | bytes 3145736 | tf_op jit(solution)/shard_map/ppermute | solution.py:18
  145.3 20.2 %collective-permute-start.10 = (bf16[256,128]{1,0:T(8,128)(2,1)S(1)}, bf16[256,128]{1,0:T(8,128)(2,1)S(1)}, u32[]{:S(2)}, u32[]{:S(2)}) collective-permute-start(bf16[256,128]{1,0:T(8,128)(2,1)S(1)} %bitcast.106), channel_id=1, source_target_pairs={{0,64},{64,0},{128,192},{192,128},{1,65},{65,1},{129,193},{193,129... | collective-permute-start | bytes 196616 | tf_op jit(solution)/shard_map/ppermute | solution.py:18
  168.8 30.2 %all-to-all-start.5 = ((bf16[64,32,128]{2,1,0:T(8,128)(2,1)}), bf16[64,32,128]{2,1,0:T(8,128)(2,1)S(1)}, u32[]{:S(2)}, u32[]{:S(2)}) async-start(bf16[64,32,128]{2,1,0:T(8,128)(2,1)} %bitcast.27), calls=%async_computation.5 | async-start | bytes 1048576 | tf_op jit(solution)/shard_map/all_to_all | solution.py:22
  199.9 27.5 %all-to-all-start.6 = ((bf16[64,32,128]{2,1,0:T(8,128)(2,1)}), bf16[64,32,128]{2,1,0:T(8,128)(2,1)}, u32[]{:S(2)}, u32[]{:S(2)}) async-start(bf16[64,32,128]{2,1,0:T(8,128)(2,1)} %fold.5), calls=%async_computation.6 | async-start | bytes 1048576 | tf_op jit(solution)/shard_map/all_to_all | solution.py:22
  207.2 24.4 %collective-permute-start.15 = (bf16[64,128]{1,0:T(8,128)(2,1)S(1)}, bf16[64,128]{1,0:T(8,128)(2,1)}, u32[]{:S(2)}, u32[]{:S(2)}) collective-permute-start(bf16[64,128]{1,0:T(8,128)(2,1)S(1)} %constant_dynamic-slice_fusion), channel_id=1, source_target_pairs={{0,64},{64,0},{128,192},{192,128},{1,65},{65,1},{129,193},{193,129... | collective-permute-start | bytes 49160 | tf_op jit(solution)/shard_map/ppermute | solution.py:18
  207.9 40.0 %collective-permute-start.23 = (bf16[256,128]{1,0:T(8,128)(2,1)}, bf16[256,128]{1,0:T(8,128)(2,1)}, u32[]{:S(2)}, u32[]{:S(2)}) collective-permute-start(bf16[256,128]{1,0:T(8,128)(2,1)} %broadcast_select_fusion.18), channel_id=1, source_target_pairs={{0,192},{64,128},{128,64},{192,0},{1,193},{65,129},{129,65},{193,1... | collective-permute-start | bytes 196616 | tf_op jit(solution)/shard_map/ppermute | solution.py:18
  211.2 20.7 %collective-permute-start.14 = (bf16[64,128]{1,0:T(8,128)(2,1)S(1)}, bf16[64,128]{1,0:T(8,128)(2,1)}, u32[]{:S(2)}, u32[]{:S(2)}) collective-permute-start(bf16[64,128]{1,0:T(8,128)(2,1)S(1)} %constant_dynamic-slice_fusion.1), channel_id=1, source_target_pairs={{0,64},{64,0},{128,192},{192,128},{1,65},{65,1},{129,193},{193,129... | collective-permute-start | bytes 49160 | tf_op jit(solution)/shard_map/ppermute | solution.py:18
  213.4 50.2 %collective-permute-start.25 = (bf16[2048,128]{1,0:T(8,128)(2,1)}, bf16[2048,128]{1,0:T(8,128)(2,1)}, u32[]{:S(2)}, u32[]{:S(2)}) collective-permute-start(bf16[2048,128]{1,0:T(8,128)(2,1)} %get-tuple-element.42), channel_id=1, source_target_pairs={{0,64},{64,0},{128,192},{192,128},{1,65},{65,1},{129,193},{193,129... | collective-permute-start | bytes 1572872 | tf_op jit(solution)/shard_map/ppermute | solution.py:18
  213.9 49.7 %collective-permute-start.26 = (bf16[2048,128]{1,0:T(8,128)(2,1)}, bf16[2048,128]{1,0:T(8,128)(2,1)}, u32[]{:S(2)}, u32[]{:S(2)}) collective-permute-start(bf16[2048,128]{1,0:T(8,128)(2,1)} %get-tuple-element.41), channel_id=1, source_target_pairs={{0,192},{64,128},{128,64},{192,0},{1,193},{65,129},{129,65},{193,1... | collective-permute-start | bytes 1572872 | tf_op jit(solution)/shard_map/ppermute | solution.py:18
  232.5 40.8 %collective-permute-start.16 = (bf16[64,128]{1,0:T(8,128)(2,1)}, bf16[64,128]{1,0:T(8,128)(2,1)}, u32[]{:S(2)}, u32[]{:S(2)}) collective-permute-start(bf16[64,128]{1,0:T(8,128)(2,1)} %select_select_fusion), channel_id=1, source_target_pairs={{0,128},{64,192},{128,0},{192,64},{1,129},{65,193},{129,1},{193,65... | collective-permute-start | bytes 49160 | tf_op jit(solution)/shard_map/ppermute | solution.py:18
  233.2 11.9 %collective-permute-start.11 = (bf16[64,128]{1,0:T(8,128)(2,1)S(1)}, bf16[64,128]{1,0:T(8,128)(2,1)S(1)}, u32[]{:S(2)}, u32[]{:S(2)}) collective-permute-start(bf16[64,128]{1,0:T(8,128)(2,1)S(1)} %constant_dynamic-slice_fusion.2), channel_id=1, source_target_pairs={{0,64},{64,0},{128,192},{192,128},{1,65},{65,1},{129,193},{193,129... | collective-permute-start | bytes 49160 | tf_op jit(solution)/shard_map/ppermute | solution.py:18
  237.5 24.8 %all-to-all-start.7 = ((bf16[64,32,128]{2,1,0:T(8,128)(2,1)}), bf16[64,32,128]{2,1,0:T(8,128)(2,1)}, u32[]{:S(2)}, u32[]{:S(2)}) async-start(bf16[64,32,128]{2,1,0:T(8,128)(2,1)} %bitcast.31), calls=%async_computation.7 | async-start | bytes 1048576 | tf_op jit(solution)/shard_map/all_to_all | solution.py:22
  245.2 4.9 %collective-permute-start.22 = (bf16[256,128]{1,0:T(8,128)(2,1)S(1)}, bf16[256,128]{1,0:T(8,128)(2,1)S(1)}, u32[]{:S(2)}, u32[]{:S(2)}) collective-permute-start(bf16[256,128]{1,0:T(8,128)(2,1)S(1)} %broadcast_select_fusion.19), channel_id=1, source_target_pairs={{0,192},{64,128},{128,64},{192,0},{1,193},{65,129},{129,65},{193,1... | collective-permute-start | bytes 196616 | tf_op jit(solution)/shard_map/ppermute | solution.py:18
  247.9 18.2 %collective-permute-start.24 = (bf16[2048,128]{1,0:T(8,128)(2,1)}, bf16[2048,128]{1,0:T(8,128)(2,1)}, u32[]{:S(2)}, u32[]{:S(2)}) collective-permute-start(bf16[2048,128]{1,0:T(8,128)(2,1)} %get-tuple-element.43), channel_id=1, source_target_pairs={{0,128},{64,192},{128,0},{192,64},{1,129},{65,193},{129,1},{193,65... | collective-permute-start | bytes 1572872 | tf_op jit(solution)/shard_map/ppermute | solution.py:18
  263.5 9.8 %collective-permute-start.13 = (bf16[32,128]{1,0:T(8,128)(2,1)S(1)}, bf16[32,128]{1,0:T(8,128)(2,1)S(1)}, u32[]{:S(2)}, u32[]{:S(2)}) collective-permute-start(bf16[32,128]{1,0:T(8,128)(2,1)S(1)} %add_convert_fusion), channel_id=1, source_target_pairs={{0,64},{64,0},{128,192},{192,128},{1,65},{65,1},{129,193},{193,129... | collective-permute-start | bytes 24584 | tf_op jit(solution)/shard_map/ppermute | solution.py:18
  (33 other events, 219.7 us)
Sparse Core Ops, SparseCore 0:
  106.3 90.5 all-gather.2

commit v2 on v1

--- a/solution.py
+++ b/solution.py
@@ -222,16 +222,17 @@
     )(place, landed, grad)
 
 
-def down_grad_kernel(mask_d, core, h, here, across, sibling, partner, out):
-    pair, i = pl.program_id(0), pl.program_id(1)
+def down_grad_kernel(choices, mask_d, info, h, *refs):
+    out, grads = refs[-1], refs[: 2 * choices]
+    i = pl.program_id(0)
     hidden, columns = out.shape[2], out.shape[3]
     pairs = hidden // BLOCK
-    half_blocks = pl.num_programs(1) * columns // BLOCK
-    layer = jnp.where(pair == 0, core[0], 1 - core[0])
+    half_blocks = pl.num_programs(0) * columns // BLOCK
+    layer = info[0]
 
     def write(a, b):
         both = jnp.concatenate([a[...], b[...]], axis=1)
-        total = lax.dot_general(h[0], both, NT, preferred_element_type=F32)
+        total = lax.dot_general(h[...], both, NT, preferred_element_type=F32)
         for k in range(columns // BLOCK):
             lanes = slice(k * BLOCK, (k + 1) * BLOCK)
             block = layer * half_blocks + i * (columns // BLOCK) + k
@@ -240,37 +241,35 @@
                 mask = mask_d[(layer * pairs + p) * 2 * half_blocks + block]
                 out[0, 0, rows, lanes] = kept_blocks(total[rows, lanes], mask).astype(BF16)
 
-    @pl.when(pair == 0)
-    def _():
-        write(here, across)
-
-    @pl.when(pair == 1)
-    def _():
-        write(sibling, partner)
-
-
-def down_grads(mask_d, core, h, here, across, sibling, partner):
-    half, tokens = here.shape
-    hidden = h.shape[1]
+    for c in range(choices):
+
+        @pl.when(info[1] == c)
+        def _(c=c):
+            write(grads[2 * c], grads[2 * c + 1])
+
+
+def down_grads(mask_d, info, h, grads, before=None):
+    half, tokens = grads[0][0].shape
+    hidden = h.shape[0]
     columns = min(512, half)
-    per = half // columns
-    first = pl.BlockSpec((columns, tokens), lambda p, i, *_: (jnp.where(p == 0, i, per - 1), 0))
-    second = pl.BlockSpec((columns, tokens), lambda p, i, *_: (jnp.where(p == 0, 0, i), 0))
-    return pl.pallas_call(
-        down_grad_kernel,
+    flat = [g for pair in grads for g in pair]
+    kept = [] if before is None else [before]
+    return pl.pallas_call(
+        functools.partial(down_grad_kernel, len(grads)),
         grid_spec=pltpu.PrefetchScalarGridSpec(
             num_scalar_prefetch=2,
-            grid=(2, per),
-            in_specs=[pl.BlockSpec((1, hidden, 2 * tokens), lambda p, i, *_: (p, 0, 0)), first, first, second, second],
-            out_specs=pl.BlockSpec(
-                (1, 1, hidden, columns), lambda p, i, _, core: (jnp.where(p == 0, core[0], 1 - core[0]), 0, 0, i)
-            ),
+            grid=(half // columns,),
+            in_specs=[pl.BlockSpec((hidden, 2 * tokens), lambda i, *_: (0, 0))]
+            + [pl.BlockSpec((columns, tokens), lambda i, *_: (i, 0))] * len(flat)
+            + [pl.BlockSpec(memory_space=pl.ANY)] * len(kept),
+            out_specs=pl.BlockSpec((1, 1, hidden, columns), lambda i, _, info: (info[0], 0, 0, i)),
         ),
         out_shape=jax.ShapeDtypeStruct((2, 1, hidden, half), BF16),
-        compiler_params=params(),
-        cost_estimate=pl.CostEstimate(flops=8 * half * hidden * tokens, bytes_accessed=8 * half * hidden, transcendentals=0),
+        input_output_aliases={3 + len(flat): 0} if kept else {},
+        compiler_params=params(),
+        cost_estimate=pl.CostEstimate(flops=4 * half * hidden * tokens, bytes_accessed=4 * half * hidden, transcendentals=0),
         name="down_grads",
-    )(mask_d, core, h, here, across, sibling, partner)
+    )(mask_d, info, h, *flat, *kept)
 
 
 def per_device(top_grad, saved_in, saved_pre, w_up, w_down, mask_up, mask_down):
@@ -356,6 +355,7 @@
 
     first_du, second_du = pick(outer, dus[3], dus[2]), pick(outer, dus[0], dus[1])
     far_first, far_second = swap(first_du, 3), swap(second_du, 3)
+    far_second, last_grad = lax.optimization_barrier((far_second, grads[0]))
     low_own, low_far = pick(near, second_du, first_du), pick(near, far_second, far_first)
     high_own, high_far = pick(near, first_du, second_du), pick(near, far_first, far_second)
     du_low = jnp.concatenate([pick(near, low_own, low_far), pick(near, low_far, low_own)], 1)
@@ -369,12 +369,18 @@
         return jnp.concatenate([pick(near, replica0, replica1), pick(near, replica1, replica0)], 1)
 
     h_low, h_high = ordered(hidden[0], hidden_far[1]), ordered(hidden_far[0], hidden[1])
-    h_pairs = jnp.stack([pick(even, h_low, h_high), pick(even, h_high, h_low)])
-    g_here = pick(outer, grads[0], grads[2])
-    g_across = swap(pick(outer, grads[2], grads[0]), 2)
     g_sibling = swap(pick(outer, grads[1], grads[3]), 1)
     g_partner = swap(pick(outer, grads[3], grads[1]), 3)
-    grad_down = down_grads(mask_d, core[None], h_pairs, g_here, g_across, g_sibling, g_partner)
+    grad_down = down_grads(
+        mask_d, jnp.stack([1 - core, zero]), pick(even, h_high, h_low), [(g_sibling, g_partner)]
+    )
+    grad_down = down_grads(
+        mask_d,
+        jnp.stack([core, outer.astype(jnp.int32)]),
+        pick(even, h_low, h_high),
+        [(grads[2], swap(grads[2], 2)), (grads[0], swap(last_grad, 2))],
+        grad_down,
+    )
     return (all_grads, grad_up, grad_down)
 
 

time: 284 us -> 303 us (1.067)
  starting transfers between devices: 72.7 us -> 90.6 us
  Pallas kernels: 32.6 us -> 36.9 us
    all_to_all x8, starting transfers between devices: 55.7 us -> 67.7 us  [exchange(): return lax.all_to_all(parts, 'tp', 0, 0, tiled=True)]
    all_to_all x8, waiting for transfers between devices: 110 us -> 102 us  [exchange(): return lax.all_to_all(parts, 'tp', 0, 0, tiled=True)]
    ppermute x24 -> x25, starting transfers between devices: 12.8 us -> 18.5 us  [swap(): return lax.ppermute(value, 'segment', [(s, s ^ bits) for s in range(4)])]
    ppermute x3, waiting for transfers between devices: 0.01 us -> 4.77 us  [per_device(): lax.ppermute(x_sent, 'tp', [(i, i ^ k * inner) for i in range(members)])]
    all_gather x1, waiting for transfers between devices: 0.01 us -> 4.4 us  [per_device(): x_full = lax.all_gather(jnp.stack(lines, 1), 'tp', axis_index_groups=groups)]
    select_n x12 -> x11, other arithmetic: 8.02 us -> 5.51 us  [pick(): return jnp.where(condition, a, b)]
    unnamed x60 -> x42, local copies, waits for them, and re-layouts: 21.2 us -> 18.9 us
    pallas_call x1 -> x2, Pallas kernels: 7.19 us -> 9.04 us  [down_grads(): pl.pallas_call(functools.partial(down_grad_kernel, len(grads)), grid_spec...]
  transfers between devices with their start and end apart: 36 -> 37, of which waited for: 16 -> 17; matrix products, arithmetic and copies ran while one was open for 6% -> 4% of each run, Pallas kernels for 11% -> 11%
where the time goes in v2:
time: 303 us; the launch traced here: 300 us
  waiting for transfers between devices  124 us (41%)
  starting transfers between devices  90.6 us (30%)
  Pallas kernels  36.9 us (12%)
  local copies, waits for them, and re-layouts  24.1 us (8%)
  between operations  14.6 us (5%)
  other arithmetic  9.3 us (3%)
    all_to_all x8, waiting for transfers between devices, exchange(): return lax.all_to_all(parts, 'tp', 0, 0, tiled=True)  102 us
    all_to_all x8, starting transfers between devices, exchange(): return lax.all_to_all(parts, 'tp', 0, 0, tiled=True)  67.7 us
    unnamed x42, local copies, waits for them, and re-layouts  18.9 us
    ppermute x25, starting transfers between devices, swap(): return lax.ppermute(value, 'segment', [(s, s ^ bits) for s in range(4)])  18.5 us
    ppermute x25, waiting for transfers between devices, swap(): return lax.ppermute(value, 'segment', [(s, s ^ bits) for s in range(4)])  12.6 us
    pallas_call x2, Pallas kernels, down_grads(): pl.pallas_call(functools.partial(down_grad_kernel, len(grads)), grid_spec...  9.04 us
    pallas_call x2, Pallas kernels, prepare(): pl.pallas_call(functools.partial(prepare_kernel, share), grid_spec=pltpu....  8.12 us
    pallas_call x4, Pallas kernels, up_step(): pl.pallas_call(up_kernel, in_specs=[pl.BlockSpec(memory_space=pltpu.SMEM)...  7.73 us
  transfers between devices with their start and end apart: 37, of which 17 were waited for; matrix products, arithmetic and copies ran while one was open for 4% of the time, Pallas kernels for 11%

profile of v2, /device:TPU:8, one launch (start us, length us, event | category | flops | bytes accessed | tf_op | source)
XLA Modules:
  0.0 299.5 jit_solution(4259260893149327785)
XLA Ops:
  8.8 13.7 %all-to-all-start = ((bf16[64,32,128]{2,1,0:T(8,128)(2,1)}), bf16[64,32,128]{2,1,0:T(8,128)(2,1)S(1)}, u32[]{:S(2)}, u32[]{:S(2)}) async-start(bf16[64,32,128]{2,1,0:T(8,128)(2,1)} %broadcast_in_dim.28), calls=%async_computation | async-start | bytes 1048576 | tf_op jit(solution)/shard_map/all_to_all | solution.py:22
  28.6 4.2 %prepare.3 = (bf16[256,2048]{1,0:T(8,128)(2,1)S(1)}, bf16[256,2048]{1,0:T(8,128)(2,1)}, bf16[2048,256]{1,0:T(8,128)(2,1)S(1)}, bf16[2048,256]{1,0:T(8,128)(2,1)}) custom-call(s32[3]{0:T(128)S(1)} %pad_add_fusion.1.info, s32[128]{0:T(128)S(1)} %reshape.59.mask_u, s32[128]{0:T(128)S(1)} %reshape.60.mask_d, bf16[2,1,4096,256]{3,2,1,0:T(8,128)(2,1)S(1)} %copy-done.1, ...), custom_call_target="tpu_custom_call" | custom-call | bytes 8388608 | tf_op jit(solution)/shard_map/prepare/pallas_call | solution.py:76
  34.3 8.2 %all-to-all-done = bf16[64,32,128]{2,1,0:T(8,128)(2,1)S(1)} async-done(((bf16[64,32,128]{2,1,0:T(8,128)(2,1)}), bf16[64,32,128]{2,1,0:T(8,128)(2,1)S(1)}, u32[]{:S(2)}, u32[]{:S(2)}) %all-to-all-start) | async-done | bytes 524320 | tf_op jit(solution)/shard_map/all_to_all | solution.py:22
  52.7 2.5 up.8
  55.2 5.1 %all-to-all-start.1 = ((bf16[64,32,128]{2,1,0:T(8,128)(2,1)}), bf16[64,32,128]{2,1,0:T(8,128)(2,1)S(1)}, u32[]{:S(2)}, u32[]{:S(2)}) async-start(bf16[64,32,128]{2,1,0:T(8,128)(2,1)} %bitcast.20), calls=%async_computation.1 | async-start | bytes 1048576 | tf_op jit(solution)/shard_map/all_to_all | solution.py:22
  60.3 19.1 %all-to-all-done.1.landed = bf16[64,32,128]{2,1,0:T(8,128)(2,1)S(1)} async-done(((bf16[64,32,128]{2,1,0:T(8,128)(2,1)}), bf16[64,32,128]{2,1,0:T(8,128)(2,1)S(1)}, u32[]{:S(2)}, u32[]{:S(2)}) %all-to-all-start.1) | async-done | bytes 524320 | tf_op jit(solution)/shard_map/all_to_all | solution.py:22
  80.4 5.5 %all-to-all-start.2 = ((bf16[64,32,128]{2,1,0:T(8,128)(2,1)}), bf16[64,32,128]{2,1,0:T(8,128)(2,1)S(1)}, u32[]{:S(2)}, u32[]{:S(2)}) async-start(bf16[64,32,128]{2,1,0:T(8,128)(2,1)} %fold.3), calls=%async_computation.2 | async-start | bytes 1048576 | tf_op jit(solution)/shard_map/all_to_all | solution.py:22
  85.9 18.9 %all-to-all-done.2 = bf16[64,32,128]{2,1,0:T(8,128)(2,1)S(1)} async-done(((bf16[64,32,128]{2,1,0:T(8,128)(2,1)}), bf16[64,32,128]{2,1,0:T(8,128)(2,1)S(1)}, u32[]{:S(2)}, u32[]{:S(2)}) %all-to-all-start.2) | async-done | bytes 524320 | tf_op jit(solution)/shard_map/all_to_all | solution.py:22
  106.7 4.0 %collective-permute-start.17 = (bf16[64,128]{1,0:T(8,128)(2,1)S(1)}, bf16[64,128]{1,0:T(8,128)(2,1)S(1)}, u32[]{:S(2)}, u32[]{:S(2)}) collective-permute-start(bf16[64,128]{1,0:T(8,128)(2,1)S(1)} %get-tuple-element.69), channel_id=1, source_target_pairs={{0,192},{64,128},{128,64},{192,0},{1,193},{65,129},{129,65},{193,1... | collective-permute-start | bytes 49160 | tf_op jit(solution)/shard_map/ppermute | solution.py:18
  113.4 5.1 %all-to-all-start.3 = ((bf16[64,32,128]{2,1,0:T(8,128)(2,1)}), bf16[64,32,128]{2,1,0:T(8,128)(2,1)S(1)}, u32[]{:S(2)}, u32[]{:S(2)}) async-start(bf16[64,32,128]{2,1,0:T(8,128)(2,1)} %bitcast.22), calls=%async_computation.3 | async-start | bytes 1048576 | tf_op jit(solution)/shard_map/all_to_all | solution.py:22
  118.7 3.3 %collective-permute-start.21 = (bf16[2,64,128]{2,1,0:T(8,128)(2,1)S(1)}, bf16[2,64,128]{2,1,0:T(8,128)(2,1)S(1)}, u32[]{:S(2)}, u32[]{:S(2)}) collective-permute-start(bf16[2,64,128]{2,1,0:T(8,128)(2,1)S(1)} %get-tuple-element.66), channel_id=1, source_target_pairs={{0,48},{1,49},{2,50},{3,51},{4,52},{5,53},{6,54},{7,55},{8,56},{9,... | collective-permute-start | bytes 98312 | tf_op jit(solution)/shard_map/ppermute | solution.py:298
  124.5 3.2 %collective-permute-done.20 = bf16[2,64,128]{2,1,0:T(8,128)(2,1)S(1)} collective-permute-done((bf16[2,64,128]{2,1,0:T(8,128)(2,1)S(1)}, bf16[2,64,128]{2,1,0:T(8,128)(2,1)S(1)}, u32[]{:S(2)}, u32[]{:S(2)}) %collective-permute-start.20) | collective-permute-done | bytes 32800 | tf_op jit(solution)/shard_map/ppermute | solution.py:298
  132.9 3.9 %prepare.2 = (bf16[256,2048]{1,0:T(8,128)(2,1)S(1)}, bf16[256,2048]{1,0:T(8,128)(2,1)}, bf16[2048,256]{1,0:T(8,128)(2,1)S(1)}, bf16[2048,256]{1,0:T(8,128)(2,1)S(1)}) custom-call(s32[3]{0:T(128)S(1)} %pad_add_fusion.info, s32[128]{0:T(128)S(1)} %reshape.59.mask_u, s32[128]{0:T(128)S(1)} %reshape.60.mask_d, bf16[2,1,4096,256]{3,2,1,0:T(8,128)(2,1)S(1)} %copy-done.2, ...), custom_call_target="tpu_custom_call" | custom-call | bytes 8388608 | tf_op jit(solution)/shard_map/prepare/pallas_call | solution.py:76
  140.0 12.0 %all-to-all-start.4 = ((bf16[64,32,128]{2,1,0:T(8,128)(2,1)}), bf16[64,32,128]{2,1,0:T(8,128)(2,1)S(1)}, u32[]{:S(2)}, u32[]{:S(2)}) async-start(bf16[64,32,128]{2,1,0:T(8,128)(2,1)} %fold.4), calls=%async_computation.4 | async-start | bytes 1048576 | tf_op jit(solution)/shard_map/all_to_all | solution.py:22
  152.8 21.5 %all-to-all-done.4 = bf16[64,32,128]{2,1,0:T(8,128)(2,1)S(1)} async-done(((bf16[64,32,128]{2,1,0:T(8,128)(2,1)}), bf16[64,32,128]{2,1,0:T(8,128)(2,1)S(1)}, u32[]{:S(2)}, u32[]{:S(2)}) %all-to-all-start.4) | async-done | bytes 524320 | tf_op jit(solution)/shard_map/all_to_all | solution.py:22
  178.3 6.8 %all-to-all-start.5 = ((bf16[64,32,128]{2,1,0:T(8,128)(2,1)}), bf16[64,32,128]{2,1,0:T(8,128)(2,1)S(1)}, u32[]{:S(2)}, u32[]{:S(2)}) async-start(bf16[64,32,128]{2,1,0:T(8,128)(2,1)} %bitcast.27), calls=%async_computation.5 | async-start | bytes 1048576 | tf_op jit(solution)/shard_map/all_to_all | solution.py:22
  185.5 20.4 %all-to-all-done.5.landed = bf16[64,32,128]{2,1,0:T(8,128)(2,1)S(1)} async-done(((bf16[64,32,128]{2,1,0:T(8,128)(2,1)}), bf16[64,32,128]{2,1,0:T(8,128)(2,1)S(1)}, u32[]{:S(2)}, u32[]{:S(2)}) %all-to-all-start.5) | async-done | bytes 524320 | tf_op jit(solution)/shard_map/all_to_all | solution.py:22
  206.8 7.0 %all-to-all-start.6 = ((bf16[64,32,128]{2,1,0:T(8,128)(2,1)}), bf16[64,32,128]{2,1,0:T(8,128)(2,1)}, u32[]{:S(2)}, u32[]{:S(2)}) async-start(bf16[64,32,128]{2,1,0:T(8,128)(2,1)} %fold.5), calls=%async_computation.6 | async-start | bytes 1048576 | tf_op jit(solution)/shard_map/all_to_all | solution.py:22
  213.9 2.8 collective-permute-start.24
  219.3 4.4 %all-gather.3.cloned.1.call-done = bf16[32,4,64,128]{3,2,0,1:T(8,128)(2,1)} async-done(((bf16[2,4,64,128]{3,2,0,1:T(8,128)(2,1)}), bf16[32,4,64,128]{3,2,0,1:T(8,128)(2,1)}) %all-gather.3.cloned.1.call-update) | async-done | bytes 2097168 | tf_op jit(solution)/shard_map/all_gather | solution.py:300
  225.5 8.6 %all-to-all-done.6 = bf16[64,32,128]{2,1,0:T(8,128)(2,1)} async-done(((bf16[64,32,128]{2,1,0:T(8,128)(2,1)}), bf16[64,32,128]{2,1,0:T(8,128)(2,1)}, u32[]{:S(2)}, u32[]{:S(2)}) %all-to-all-start.6) | async-done | bytes 524320 | tf_op jit(solution)/shard_map/all_to_all | solution.py:22
  235.3 2.7 down.11.part
  240.4 2.8 collective-permute-done.27.refs_1_
  243.2 4.4 %down_grads.2.refs_4_ = bf16[2,1,256,2048]{3,2,1,0:T(8,128)(2,1)} custom-call(s32[128]{0:T(128)S(1)} %reshape.60.mask_d, s32[2]{0:T(128)S(1)} %pad_add_fusion.3.info, bf16[256,256]{1,0:T(8,128)(2,1)S(1)} %get-tuple-element.49.h, bf16[2048,128]{1,0:T(8,128)(2,1)} %collective-permute-done.26.refs_0_, bf16[2048,128]{1,0:T(8,128)(2,1)} %collective-permute-done.27.refs_1_), custom_call_target="tpu_custom_call" | custom-call | flops 268435456 | bytes 2097152 | tf_op jit(solution)/shard_map/down_grads/pallas_call | solution.py:257
  247.6 2.5 up.11
  250.2 12.4 %all-to-all-start.7 = ((bf16[64,32,128]{2,1,0:T(8,128)(2,1)}), bf16[64,32,128]{2,1,0:T(8,128)(2,1)}, u32[]{:S(2)}, u32[]{:S(2)}) async-start(bf16[64,32,128]{2,1,0:T(8,128)(2,1)} %bitcast.31), calls=%async_computation.7 | async-start | bytes 1048576 | tf_op jit(solution)/shard_map/all_to_all | solution.py:22
  266.3 2.4 collective-permute-done.22
  268.7 2.4 collective-permute-start.25
  272.0 4.9 %up_grads.1 = bf16[2,1,2048,256]{3,2,1,0:T(8,128)(2,1)} custom-call(s32[128]{0:T(128)S(1)} %reshape.59.mask_u, s32[1]{0:T(128)} %bitcast.37.line, bf16[16,2,4,64,128]{4,3,2,1,0:T(8,128)(2,1)S(1)} %bitcast.107, bf16[2,256,256]{2,1,0:T(8,128)(2,1)S(1)} %pad_maximum_fusion.du), custom_call_target="tpu_custom_call" | custom-call | flops 536870912 | bytes 4194304 | tf_op jit(solution)/shard_map/up_grads/pallas_call | solution.py:179
  277.0 5.4 %all-to-all-done.7 = bf16[64,32,128]{2,1,0:T(8,128)(2,1)} async-done(((bf16[64,32,128]{2,1,0:T(8,128)(2,1)}), bf16[64,32,128]{2,1,0:T(8,128)(2,1)}, u32[]{:S(2)}, u32[]{:S(2)}) %all-to-all-start.7) | async-done | bytes 524320 | tf_op jit(solution)/shard_map/all_to_all | solution.py:22
  283.7 3.0 %collective-permute-done.25.refs_3_ = bf16[2048,128]{1,0:T(8,128)(2,1)} collective-permute-done((bf16[2048,128]{1,0:T(8,128)(2,1)}, bf16[2048,128]{1,0:T(8,128)(2,1)}, u32[]{:S(2)}, u32[]{:S(2)}) %collective-permute-start.25) | collective-permute-done | bytes 524320 | tf_op jit(solution)/shard_map/ppermute | solution.py:18
  286.7 4.6 %down_grads.3 = bf16[2,1,256,2048]{3,2,1,0:T(8,128)(2,1)} custom-call(s32[128]{0:T(128)S(1)} %reshape.60.mask_d, s32[2]{0:T(128)S(1)} %pad_add_fusion.2.info, bf16[256,256]{1,0:T(8,128)(2,1)S(1)} %get-tuple-element.50.h, bf16[2048,128]{1,0:T(8,128)(2,1)S(1)} %bitcast.106, ...), custom_call_target="tpu_custom_call", output_to_operand_aliasing={{}: (7, {})} | custom-call | flops 268435456 | bytes 2097152 | tf_op jit(solution)/shard_map/down_grads/pallas_call | solution.py:257
  (141 shorter events, 57.2 us)
Async XLA Ops:
  8.8 33.7 %all-to-all-start = ((bf16[64,32,128]{2,1,0:T(8,128)(2,1)}), bf16[64,32,128]{2,1,0:T(8,128)(2,1)S(1)}, u32[]{:S(2)}, u32[]{:S(2)}) async-start(bf16[64,32,128]{2,1,0:T(8,128)(2,1)} %broadcast_in_dim.28), calls=%async_computation | async-start | bytes 1048576 | tf_op jit(solution)/shard_map/all_to_all | solution.py:22
  33.8 12.7 %collective-permute-start.3 = (bf16[256,2048]{1,0:T(8,128)(2,1)}, bf16[256,2048]{1,0:T(8,128)(2,1)S(1)}, u32[]{:S(2)}, u32[]{:S(2)}) collective-permute-start(bf16[256,2048]{1,0:T(8,128)(2,1)} %get-tuple-element.28), channel_id=1, source_target_pairs={{0,64},{64,0},{128,192},{192,128},{1,65},{65,1},{129,193},{193,129... | collective-permute-start | bytes 3145736 | tf_op jit(solution)/shard_map/ppermute | solution.py:18
  33.8 17.7 %collective-permute-start.2 = (bf16[2048,256]{1,0:T(8,128)(2,1)}, bf16[2048,256]{1,0:T(8,128)(2,1)}, u32[]{:S(2)}, u32[]{:S(2)}) collective-permute-start(bf16[2048,256]{1,0:T(8,128)(2,1)} %get-tuple-element.26), channel_id=1, source_target_pairs={{0,64},{64,0},{128,192},{192,128},{1,65},{65,1},{129,193},{193,129... | collective-permute-start | bytes 3145736 | tf_op jit(solution)/shard_map/ppermute | solution.py:18
  43.4 5.0 %collective-permute-start.7 = (bf16[256,128]{1,0:T(8,128)(2,1)}, bf16[256,128]{1,0:T(8,128)(2,1)}, u32[]{:S(2)}, u32[]{:S(2)}) collective-permute-start(bf16[256,128]{1,0:T(8,128)(2,1)} %bitcast.19), channel_id=1, source_target_pairs={{0,128},{64,192},{128,0},{192,64},{1,129},{65,193},{129,1},{193,65... | collective-permute-start | bytes 196616 | tf_op jit(solution)/shard_map/ppermute | solution.py:18
  44.8 5.8 %collective-permute-start.6 = (bf16[2,256,128]{2,1,0:T(8,128)(2,1)S(1)}, bf16[2,256,128]{2,1,0:T(8,128)(2,1)S(1)}, u32[]{:S(2)}, u32[]{:S(2)}) collective-permute-start(bf16[2,256,128]{2,1,0:T(8,128)(2,1)S(1)} %bitcast.111), channel_id=1, source_target_pairs={{0,192},{64,128},{128,64},{192,0},{1,193},{65,129},{129,65},{193,1... | collective-permute-start | bytes 393224 | tf_op jit(solution)/shard_map/ppermute | solution.py:18
  55.2 24.3 %all-to-all-start.1 = ((bf16[64,32,128]{2,1,0:T(8,128)(2,1)}), bf16[64,32,128]{2,1,0:T(8,128)(2,1)S(1)}, u32[]{:S(2)}, u32[]{:S(2)}) async-start(bf16[64,32,128]{2,1,0:T(8,128)(2,1)} %bitcast.20), calls=%async_computation.1 | async-start | bytes 1048576 | tf_op jit(solution)/shard_map/all_to_all | solution.py:22
  80.4 24.4 %all-to-all-start.2 = ((bf16[64,32,128]{2,1,0:T(8,128)(2,1)}), bf16[64,32,128]{2,1,0:T(8,128)(2,1)S(1)}, u32[]{:S(2)}, u32[]{:S(2)}) async-start(bf16[64,32,128]{2,1,0:T(8,128)(2,1)} %fold.3), calls=%async_computation.2 | async-start | bytes 1048576 | tf_op jit(solution)/shard_map/all_to_all | solution.py:22
  106.7 11.9 %collective-permute-start.17 = (bf16[64,128]{1,0:T(8,128)(2,1)S(1)}, bf16[64,128]{1,0:T(8,128)(2,1)S(1)}, u32[]{:S(2)}, u32[]{:S(2)}) collective-permute-start(bf16[64,128]{1,0:T(8,128)(2,1)S(1)} %get-tuple-element.69), channel_id=1, source_target_pairs={{0,192},{64,128},{128,64},{192,0},{1,193},{65,129},{129,65},{193,1... | collective-permute-start | bytes 49160 | tf_op jit(solution)/shard_map/ppermute | solution.py:18
  110.7 7.9 %collective-permute-start.18 = (bf16[64,128]{1,0:T(8,128)(2,1)S(1)}, bf16[64,128]{1,0:T(8,128)(2,1)S(1)}, u32[]{:S(2)}, u32[]{:S(2)}) collective-permute-start(bf16[64,128]{1,0:T(8,128)(2,1)S(1)} %get-tuple-element.70), channel_id=1, source_target_pairs={{0,192},{64,128},{128,64},{192,0},{1,193},{65,129},{129,65},{193,1... | collective-permute-start | bytes 49160 | tf_op jit(solution)/shard_map/ppermute | solution.py:18
  113.4 25.6 %all-to-all-start.3 = ((bf16[64,32,128]{2,1,0:T(8,128)(2,1)}), bf16[64,32,128]{2,1,0:T(8,128)(2,1)S(1)}, u32[]{:S(2)}, u32[]{:S(2)}) async-start(bf16[64,32,128]{2,1,0:T(8,128)(2,1)} %bitcast.22), calls=%async_computation.3 | async-start | bytes 1048576 | tf_op jit(solution)/shard_map/all_to_all | solution.py:22
  118.5 105.1 %all-gather.3.cloned.1.call-start = ((), (), s32[]{:S(2)}) async-start(), calls=%async_computation.8 | async-start | bytes 2228224 | tf_op jit(solution)/shard_map/all_gather | solution.py:300
  118.7 5.9 %collective-permute-start.21 = (bf16[2,64,128]{2,1,0:T(8,128)(2,1)S(1)}, bf16[2,64,128]{2,1,0:T(8,128)(2,1)S(1)}, u32[]{:S(2)}, u32[]{:S(2)}) collective-permute-start(bf16[2,64,128]{2,1,0:T(8,128)(2,1)S(1)} %get-tuple-element.66), channel_id=1, source_target_pairs={{0,48},{1,49},{2,50},{3,51},{4,52},{5,53},{6,54},{7,55},{8,56},{9,... | collective-permute-start | bytes 98312 | tf_op jit(solution)/shard_map/ppermute | solution.py:298
  121.9 5.9 %collective-permute-start.20 = (bf16[2,64,128]{2,1,0:T(8,128)(2,1)S(1)}, bf16[2,64,128]{2,1,0:T(8,128)(2,1)S(1)}, u32[]{:S(2)}, u32[]{:S(2)}) collective-permute-start(bf16[2,64,128]{2,1,0:T(8,128)(2,1)S(1)} %get-tuple-element.66), channel_id=1, source_target_pairs={{0,32},{1,33},{2,34},{3,35},{4,36},{5,37},{6,38},{7,39},{8,40},{9,... | collective-permute-start | bytes 98312 | tf_op jit(solution)/shard_map/ppermute | solution.py:298
  122.6 5.2 %collective-permute-start.19 = (bf16[2,64,128]{2,1,0:T(8,128)(2,1)S(1)}, bf16[2,64,128]{2,1,0:T(8,128)(2,1)S(1)}, u32[]{:S(2)}, u32[]{:S(2)}) collective-permute-start(bf16[2,64,128]{2,1,0:T(8,128)(2,1)S(1)} %get-tuple-element.66), channel_id=1, source_target_pairs={{0,16},{1,17},{2,18},{3,19},{4,20},{5,21},{6,22},{7,23},{8,24},{9,... | collective-permute-start | bytes 98312 | tf_op jit(solution)/shard_map/ppermute | solution.py:298
  138.8 14.0 %collective-permute-start.1 = (bf16[256,2048]{1,0:T(8,128)(2,1)}, bf16[256,2048]{1,0:T(8,128)(2,1)}, u32[]{:S(2)}, u32[]{:S(2)}) collective-permute-start(bf16[256,2048]{1,0:T(8,128)(2,1)} %get-tuple-element.24), channel_id=1, source_target_pairs={{0,64},{64,0},{128,192},{192,128},{1,65},{65,1},{129,193},{193,129... | collective-permute-start | bytes 3145736 | tf_op jit(solution)/shard_map/ppermute | solution.py:18
  140.0 34.3 %all-to-all-start.4 = ((bf16[64,32,128]{2,1,0:T(8,128)(2,1)}), bf16[64,32,128]{2,1,0:T(8,128)(2,1)S(1)}, u32[]{:S(2)}, u32[]{:S(2)}) async-start(bf16[64,32,128]{2,1,0:T(8,128)(2,1)} %fold.4), calls=%async_computation.4 | async-start | bytes 1048576 | tf_op jit(solution)/shard_map/all_to_all | solution.py:22
  152.0 22.9 %collective-permute-start = (bf16[2048,256]{1,0:T(8,128)(2,1)}, bf16[2048,256]{1,0:T(8,128)(2,1)}, u32[]{:S(2)}, u32[]{:S(2)}) collective-permute-start(bf16[2048,256]{1,0:T(8,128)(2,1)} %copy-done.17), channel_id=1, source_target_pairs={{0,64},{64,0},{128,192},{192,128},{1,65},{65,1},{129,193},{193,129... | collective-permute-start | bytes 3145736 | tf_op jit(solution)/shard_map/ppermute | solution.py:18
  152.4 22.5 %collective-permute-start.10 = (bf16[256,128]{1,0:T(8,128)(2,1)S(1)}, bf16[256,128]{1,0:T(8,128)(2,1)S(1)}, u32[]{:S(2)}, u32[]{:S(2)}) collective-permute-start(bf16[256,128]{1,0:T(8,128)(2,1)S(1)} %bitcast.112), channel_id=1, source_target_pairs={{0,64},{64,0},{128,192},{192,128},{1,65},{65,1},{129,193},{193,129... | collective-permute-start | bytes 196616 | tf_op jit(solution)/shard_map/ppermute | solution.py:18
  178.3 27.6 %all-to-all-start.5 = ((bf16[64,32,128]{2,1,0:T(8,128)(2,1)}), bf16[64,32,128]{2,1,0:T(8,128)(2,1)S(1)}, u32[]{:S(2)}, u32[]{:S(2)}) async-start(bf16[64,32,128]{2,1,0:T(8,128)(2,1)} %bitcast.27), calls=%async_computation.5 | async-start | bytes 1048576 | tf_op jit(solution)/shard_map/all_to_all | solution.py:22
  206.8 27.3 %all-to-all-start.6 = ((bf16[64,32,128]{2,1,0:T(8,128)(2,1)}), bf16[64,32,128]{2,1,0:T(8,128)(2,1)}, u32[]{:S(2)}, u32[]{:S(2)}) async-start(bf16[64,32,128]{2,1,0:T(8,128)(2,1)} %fold.5), calls=%async_computation.6 | async-start | bytes 1048576 | tf_op jit(solution)/shard_map/all_to_all | solution.py:22
  213.9 69.8 %collective-permute-start.24 = (bf16[2048,128]{1,0:T(8,128)(2,1)S(1)}, bf16[2048,128]{1,0:T(8,128)(2,1)}, u32[]{:S(2)}, u32[]{:S(2)}) collective-permute-start(bf16[2048,128]{1,0:T(8,128)(2,1)S(1)} %bitcast.103), channel_id=1, source_target_pairs={{0,128},{64,192},{128,0},{192,64},{1,129},{65,193},{129,1},{193,65... | collective-permute-start | bytes 1572872 | tf_op jit(solution)/shard_map/ppermute | solution.py:18
  216.7 21.3 %collective-permute-start.15 = (bf16[64,128]{1,0:T(8,128)(2,1)S(1)}, bf16[64,128]{1,0:T(8,128)(2,1)}, u32[]{:S(2)}, u32[]{:S(2)}) collective-permute-start(bf16[64,128]{1,0:T(8,128)(2,1)S(1)} %constant_dynamic-slice_fusion), channel_id=1, source_target_pairs={{0,64},{64,0},{128,192},{192,128},{1,65},{65,1},{129,193},{193,129... | collective-permute-start | bytes 49160 | tf_op jit(solution)/shard_map/ppermute | solution.py:18
  217.9 20.7 %collective-permute-start.26 = (bf16[2048,128]{1,0:T(8,128)(2,1)}, bf16[2048,128]{1,0:T(8,128)(2,1)}, u32[]{:S(2)}, u32[]{:S(2)}) collective-permute-start(bf16[2048,128]{1,0:T(8,128)(2,1)} %get-tuple-element.46), channel_id=1, source_target_pairs={{0,64},{64,0},{128,192},{192,128},{1,65},{65,1},{129,193},{193,129... | collective-permute-start | bytes 1572872 | tf_op jit(solution)/shard_map/ppermute | solution.py:18
  218.4 24.8 %collective-permute-start.27 = (bf16[2048,128]{1,0:T(8,128)(2,1)}, bf16[2048,128]{1,0:T(8,128)(2,1)}, u32[]{:S(2)}, u32[]{:S(2)}) collective-permute-start(bf16[2048,128]{1,0:T(8,128)(2,1)} %get-tuple-element.45), channel_id=1, source_target_pairs={{0,192},{64,128},{128,64},{192,0},{1,193},{65,129},{129,65},{193,1... | collective-permute-start | bytes 1572872 | tf_op jit(solution)/shard_map/ppermute | solution.py:18
  218.4 19.8 %collective-permute-start.14 = (bf16[64,128]{1,0:T(8,128)(2,1)S(1)}, bf16[64,128]{1,0:T(8,128)(2,1)}, u32[]{:S(2)}, u32[]{:S(2)}) collective-permute-start(bf16[64,128]{1,0:T(8,128)(2,1)S(1)} %constant_dynamic-slice_fusion.1), channel_id=1, source_target_pairs={{0,64},{64,0},{128,192},{192,128},{1,65},{65,1},{129,193},{193,129... | collective-permute-start | bytes 49160 | tf_op jit(solution)/shard_map/ppermute | solution.py:18
  238.1 33.0 %collective-permute-start.23 = (bf16[256,128]{1,0:T(8,128)(2,1)}, bf16[256,128]{1,0:T(8,128)(2,1)}, u32[]{:S(2)}, u32[]{:S(2)}) collective-permute-start(bf16[256,128]{1,0:T(8,128)(2,1)} %broadcast_select_fusion.12), channel_id=1, source_target_pairs={{0,192},{64,128},{128,64},{192,0},{1,193},{65,129},{129,65},{193,1... | collective-permute-start | bytes 196616 | tf_op jit(solution)/shard_map/ppermute | solution.py:18
  238.2 9.5 %collective-permute-start.12 = (f32[256,128]{1,0:T(8,128)S(1)}, f32[256,128]{1,0:T(8,128)S(1)}, u32[]{:S(2)}, u32[]{:S(2)}) collective-permute-start(f32[256,128]{1,0:T(8,128)S(1)} %down.11.part), channel_id=1, source_target_pairs={{0,64},{64,0},{128,192},{192,128},{1,65},{65,1},{129,193},{193,129... | collective-permute-start | bytes 393224 | tf_op jit(solution)/shard_map/ppermute | solution.py:18
  238.5 52.7 %collective-permute-start.16 = (bf16[64,128]{1,0:T(8,128)(2,1)S(1)}, bf16[64,128]{1,0:T(8,128)(2,1)}, u32[]{:S(2)}, u32[]{:S(2)}) collective-permute-start(bf16[64,128]{1,0:T(8,128)(2,1)S(1)} %select_select_fusion), channel_id=1, source_target_pairs={{0,128},{64,192},{128,0},{192,64},{1,129},{65,193},{129,1},{193,65... | collective-permute-start | bytes 49160 | tf_op jit(solution)/shard_map/ppermute | solution.py:18
  250.2 32.2 %all-to-all-start.7 = ((bf16[64,32,128]{2,1,0:T(8,128)(2,1)}), bf16[64,32,128]{2,1,0:T(8,128)(2,1)}, u32[]{:S(2)}, u32[]{:S(2)}) async-start(bf16[64,32,128]{2,1,0:T(8,128)(2,1)} %bitcast.31), calls=%async_computation.7 | async-start | bytes 1048576 | tf_op jit(solution)/shard_map/all_to_all | solution.py:22
  263.3 5.4 %collective-permute-start.22 = (bf16[256,128]{1,0:T(8,128)(2,1)S(1)}, bf16[256,128]{1,0:T(8,128)(2,1)S(1)}, u32[]{:S(2)}, u32[]{:S(2)}) collective-permute-start(bf16[256,128]{1,0:T(8,128)(2,1)S(1)} %broadcast_select_fusion.13), channel_id=1, source_target_pairs={{0,192},{64,128},{128,64},{192,0},{1,193},{65,129},{129,65},{193,1... | collective-permute-start | bytes 196616 | tf_op jit(solution)/shard_map/ppermute | solution.py:18
  268.7 18.0 %collective-permute-start.25 = (bf16[2048,128]{1,0:T(8,128)(2,1)}, bf16[2048,128]{1,0:T(8,128)(2,1)}, u32[]{:S(2)}, u32[]{:S(2)}) collective-permute-start(bf16[2048,128]{1,0:T(8,128)(2,1)} %bitcast.28.grad.refs_2_), channel_id=1, source_target_pairs={{0,128},{64,192},{128,0},{192,64},{1,129},{65,193},{129,1},{193,65... | collective-permute-start | bytes 1572872 | tf_op jit(solution)/shard_map/ppermute | solution.py:18
  283.5 7.7 %collective-permute-start.13 = (bf16[32,128]{1,0:T(8,128)(2,1)S(1)}, bf16[32,128]{1,0:T(8,128)(2,1)S(1)}, u32[]{:S(2)}, u32[]{:S(2)}) collective-permute-start(bf16[32,128]{1,0:T(8,128)(2,1)S(1)} %add_convert_fusion), channel_id=1, source_target_pairs={{0,64},{64,0},{128,192},{192,128},{1,65},{65,1},{129,193},{193,129... | collective-permute-start | bytes 24584 | tf_op jit(solution)/shard_map/ppermute | solution.py:18
  (25 other events, 146.4 us)
Sparse Core Ops, SparseCore 0:
  128.6 95.0 all-gather.2
